TPU v7x, 256 devices: a whole 4x4x8 slice. The times are simulated.
256 devices in a mesh: seq: 32 (over x, y, core), head: 8 (over z).
Axes of the slice: x: 4, y: 4, z: 8, core: 2. Of those that a mesh axis runs over, the one named last changes fastest.
Arguments:
- query_heads: bfloat16 [8192, 4096], P('seq', 'head'), may hold values from -6 to 6
- key_heads: bfloat16 [8192, 1024], P('seq', 'head'), may hold values from -6 to 6
- value_heads: bfloat16 [8192, 1024], P('seq', 'head'), may hold values from -6 to 6
- attention_out: bfloat16 [8192, 4096], P('seq', 'head'), may hold values from -6 to 6
- log_norm: float32 [32, 8192], P('head', 'seq'), as said below
- upstream: bfloat16 [8192, 4096], P('seq', 'head'), may hold values from -6 to 6
- output_weight: bfloat16 [4096, 4096], P('head'), may hold values from -0.09375 to 0.09375
- document_lengths: int32 [8], replicated, may hold values from 1 to 4096, as said below
- block_owners: int32 [64], replicated, may hold values from 0 to 63, each once
Outputs:
- query_grad: bfloat16 [8192, 4096], P('seq', 'head')
- key_grad: bfloat16 [8192, 1024], P('seq', 'head')
- value_grad: bfloat16 [8192, 1024], P('seq', 'head')
Inputs may be any that keep to these rules, and one draw needn't show every extreme that they name: `document_lengths`: they sum to 8192; exactly one document has 4096 tokens. `block_owners`: A permutation: every row block is named once. log_norm[h, r] is the log of the sum over s with allowed(r, s) = 1 of exp(scores[h, r, s]).
All inputs are finite; a program needn't handle non-finite values.
Results may differ from a plain program's by a relative error of at most 0.013.
Values may be sent and summed in bfloat16 or wider, within the bound.
No kernel may reach another device: no remote copies, remote signals or barrier semaphores. Data moves between devices by JAX's collectives and lax.ppermute only.
A program may use at most 64 MiB of HBM per device.

v0:
```python
import math

import jax
import jax.numpy as jnp
from jax import lax
from jax.sharding import PartitionSpec as P

HD = 128


def shifted(value, axis, by):
    peers = lax.axis_size(axis)
    return lax.ppermute(value, axis, [(i, (i + by) % peers) for i in range(peers)])


def row_position(row_index, half_rows, cycle_size):
    row_block = row_index // half_rows
    device = row_block // 2
    target = jnp.where(row_block % 2 == 0, device, 2 * cycle_size - 1 - device)
    return target * half_rows + row_index % half_rows


def document_of(positions, document_lengths):
    doc_ends = jnp.cumsum(document_lengths)
    return jnp.sum((doc_ends[None, :] <= positions[:, None]).astype(jnp.int32), axis=1)


def tile_mask(query_pos, query_doc, key_pos, key_doc):
    return (key_pos[None, :] <= query_pos[:, None]) & (key_doc[None, :] == query_doc[:, None])


def tile_scores(queries, key_rows, factor):
    return (
        jnp.einsum("qcgd,kcd->cgqk", queries, key_rows, preferred_element_type=jnp.float32) * factor
    )


def grad_tile(query_part, key_part, factor):
    queries, out_grad, norms, row_delta, query_pos, query_doc = query_part
    key_rows, value_rows, key_pos, key_doc = key_part
    scores = tile_scores(queries, key_rows, factor)
    allowed = tile_mask(query_pos, query_doc, key_pos, key_doc)
    weights = jnp.where(allowed, jnp.exp(scores - norms[..., None]), 0.0)
    value_part = jnp.einsum(
        "cgqk,qcgd->kcd", weights.astype(jnp.bfloat16), out_grad, preferred_element_type=jnp.float32
    )
    prob_grad = jnp.einsum(
        "qcgd,kcd->cgqk", out_grad, value_rows, preferred_element_type=jnp.float32
    )
    score_grad = (weights * (prob_grad - row_delta[..., None])).astype(jnp.bfloat16)
    query_add = (
        jnp.einsum("cgqk,kcd->qcgd", score_grad, key_rows, preferred_element_type=jnp.float32)
        * factor
    )
    key_add = (
        jnp.einsum("cgqk,qcgd->kcd", score_grad, queries, preferred_element_type=jnp.float32)
        * factor
    )
    return (query_add, key_add, value_part)


def block_grads(query_part, key_part, factor):
    return grad_tile(query_part, key_part, factor)


def per_device(
    query_heads,
    key_heads,
    value_heads,
    attention_out,
    log_norm,
    upstream,
    output_weight,
    document_lengths,
    block_owners,
):
    cycle_size = lax.axis_size("seq")
    my_index = lax.axis_index("seq")
    tok_rows = query_heads.shape[0]
    half_rows = tok_rows // 2
    kv_local = key_heads.shape[1] // HD
    group_size = query_heads.shape[1] // key_heads.shape[1]
    factor = 1.0 / math.sqrt(HD)
    queries = query_heads.reshape(tok_rows, kv_local, group_size, HD)
    key_rows = key_heads.reshape(tok_rows, kv_local, HD)
    value_rows = value_heads.reshape(tok_rows, kv_local, HD)
    norms = log_norm.reshape(kv_local, group_size, tok_rows)
    base_rows = jnp.arange(tok_rows, dtype=jnp.int32)
    query_pos = row_position(my_index * tok_rows + base_rows, half_rows, cycle_size)
    query_doc = document_of(query_pos, document_lengths)
    out_grad = lax.dot_general(
        lax.all_gather(upstream, "head", axis=1, tiled=True),
        output_weight,
        (((1,), (1,)), ((), ())),
        preferred_element_type=jnp.float32,
    ).astype(jnp.bfloat16)
    out_grad = out_grad.reshape(tok_rows, kv_local, group_size, HD)
    products = out_grad.astype(jnp.float32) * attention_out.reshape(
        tok_rows, kv_local, group_size, HD
    ).astype(jnp.float32)
    row_delta = jnp.transpose(jnp.sum(products, axis=-1), (1, 2, 0))
    query_part = (queries, out_grad, norms, row_delta, query_pos, query_doc)
    kv_pair = jnp.stack([key_rows, value_rows], axis=0)

    def key_info(source):
        key_pos = row_position(source * tok_rows + base_rows, half_rows, cycle_size)
        return (key_pos, document_of(key_pos, document_lengths))

    def grad_turn(turn_index, loop_state):
        query_total, visiting, partial_sums = loop_state
        key_pos, key_doc = key_info((my_index - turn_index) % cycle_size)
        gradients = block_grads(query_part, (visiting[0], visiting[1], key_pos, key_doc), factor)
        partial_sums = partial_sums + jnp.stack([gradients[1], gradients[2]], axis=0)
        visiting = shifted(visiting, "seq", 1)
        partial_sums = shifted(partial_sums, "seq", 1)
        return (query_total + gradients[0], visiting, partial_sums)

    start_grads = (
        jnp.zeros((tok_rows, kv_local, group_size, HD), jnp.float32),
        kv_pair,
        jnp.zeros((2, tok_rows, kv_local, HD), jnp.float32),
    )
    query_total, visiting, partial_sums = lax.fori_loop(0, cycle_size, grad_turn, start_grads)
    key_final = partial_sums[0]
    value_final = partial_sums[1]
    width = kv_local * HD
    finished = jnp.concatenate(
        [key_final.reshape(tok_rows, width), value_final.reshape(tok_rows, width)], axis=1
    ).astype(jnp.bfloat16)
    empty_blocks = jnp.zeros((2, half_rows, 2 * width), jnp.bfloat16)
    shards = lax.all_gather(finished, "seq", axis=0, tiled=True)
    chosen_blocks = []
    for slot_index in range(2):
        source_row = block_owners[2 * my_index + slot_index] * half_rows
        inside = (source_row >= 0) & (source_row < shards.shape[0])
        chosen = lax.dynamic_slice_in_dim(
            shards, jnp.clip(source_row, 0, shards.shape[0] - half_rows), half_rows, 0
        )
        chosen_blocks.append(jnp.where(inside, chosen, empty_blocks[slot_index]))
    collected = jnp.stack(chosen_blocks, axis=0)
    collected = collected.reshape(tok_rows, 2 * width)
    query_grad = query_total.astype(jnp.bfloat16).reshape(tok_rows, kv_local * group_size * HD)
    return (query_grad, collected[:, :width], collected[:, width:])


def solution(mesh):
    placed = (
        P("seq", "head"),
        P("seq", "head"),
        P("seq", "head"),
        P("seq", "head"),
        P("head", "seq"),
        P("seq", "head"),
        P("head", None),
        P(),
        P(),
    )
    return jax.shard_map(
        per_device,
        mesh=mesh,
        in_specs=placed,
        out_specs=(P("seq", "head"), P("seq", "head"), P("seq", "head")),
        check_vma=False,
    )
```

profile of v0, /device:TPU:1, one launch (start us, length us, event | category | flops | bytes accessed | tf_op | source)
XLA Modules:
  0.0 464.5 jit_solution(12444338684356240631)
XLA Ops:
  12.2 38.9 %all-gather.3.cloned.1.call-done = bf16[256,4096]{1,0:T(8,128)(2,1)} async-done(((bf16[256,512]{1,0:T(8,128)(2,1)}), bf16[256,4096]{1,0:T(8,128)(2,1)}) %all-gather.3.cloned.1.call-update) | async-done | bytes 2097168 | tf_op jit(solution)/shard_map/all_gather | solution.py:92
  55.8 346.6 %while.21 = (s32[]{:T(128)}, f32[256,1,4,128]{3,0,2,1:T(8,128)S(1)}, bf16[2,256,1,128]{3,1,2,0:T(8,128)(2,1)S(1)}, f32[2,256,1,128]{3,1,2,0:T(8,128)S(1)}, s32[]...) while((s32[]{:T(128)}, ...), condition=%wide.region_5.6_spmd.clone, body=%wide.region_3.5_spmd.clone.sunk | while | flops 338161408 | bytes 10043812 | solution.py:123
  98.2 6.7 %collective-permute-done = bf16[2,256,1,128]{3,1,2,0:T(8,128)(2,1)S(1)} collective-permute-done((bf16[2,256,1,128]{3,1,2,0:T(8,128)(2,1)S(1)}, bf16[2,256,1,128]{3,1,2,0:T(8,128)(2,1)S(1)}, u32[]{:S(2)}, u32[]{:S(2)}) %collective-permute-start) | collective-permute-done | bytes 131104 | tf_op jit(solution)/shard_map/while/body/eval_jaxpr/ppermute | solution.py:13
  109.1 6.7 %collective-permute-done = bf16[2,256,1,128]{3,1,2,0:T(8,128)(2,1)S(1)} collective-permute-done((bf16[2,256,1,128]{3,1,2,0:T(8,128)(2,1)S(1)}, bf16[2,256,1,128]{3,1,2,0:T(8,128)(2,1)S(1)}, u32[]{:S(2)}, u32[]{:S(2)}) %collective-permute-start) | collective-permute-done | bytes 131104 | tf_op jit(solution)/shard_map/while/body/eval_jaxpr/ppermute | solution.py:13
  120.0 6.7 %collective-permute-done = bf16[2,256,1,128]{3,1,2,0:T(8,128)(2,1)S(1)} collective-permute-done((bf16[2,256,1,128]{3,1,2,0:T(8,128)(2,1)S(1)}, bf16[2,256,1,128]{3,1,2,0:T(8,128)(2,1)S(1)}, u32[]{:S(2)}, u32[]{:S(2)}) %collective-permute-start) | collective-permute-done | bytes 131104 | tf_op jit(solution)/shard_map/while/body/eval_jaxpr/ppermute | solution.py:13
  131.0 6.7 %collective-permute-done = bf16[2,256,1,128]{3,1,2,0:T(8,128)(2,1)S(1)} collective-permute-done((bf16[2,256,1,128]{3,1,2,0:T(8,128)(2,1)S(1)}, bf16[2,256,1,128]{3,1,2,0:T(8,128)(2,1)S(1)}, u32[]{:S(2)}, u32[]{:S(2)}) %collective-permute-start) | collective-permute-done | bytes 131104 | tf_op jit(solution)/shard_map/while/body/eval_jaxpr/ppermute | solution.py:13
  141.9 6.7 %collective-permute-done = bf16[2,256,1,128]{3,1,2,0:T(8,128)(2,1)S(1)} collective-permute-done((bf16[2,256,1,128]{3,1,2,0:T(8,128)(2,1)S(1)}, bf16[2,256,1,128]{3,1,2,0:T(8,128)(2,1)S(1)}, u32[]{:S(2)}, u32[]{:S(2)}) %collective-permute-start) | collective-permute-done | bytes 131104 | tf_op jit(solution)/shard_map/while/body/eval_jaxpr/ppermute | solution.py:13
  152.9 6.7 %collective-permute-done = bf16[2,256,1,128]{3,1,2,0:T(8,128)(2,1)S(1)} collective-permute-done((bf16[2,256,1,128]{3,1,2,0:T(8,128)(2,1)S(1)}, bf16[2,256,1,128]{3,1,2,0:T(8,128)(2,1)S(1)}, u32[]{:S(2)}, u32[]{:S(2)}) %collective-permute-start) | collective-permute-done | bytes 131104 | tf_op jit(solution)/shard_map/while/body/eval_jaxpr/ppermute | solution.py:13
  163.8 6.7 %collective-permute-done = bf16[2,256,1,128]{3,1,2,0:T(8,128)(2,1)S(1)} collective-permute-done((bf16[2,256,1,128]{3,1,2,0:T(8,128)(2,1)S(1)}, bf16[2,256,1,128]{3,1,2,0:T(8,128)(2,1)S(1)}, u32[]{:S(2)}, u32[]{:S(2)}) %collective-permute-start) | collective-permute-done | bytes 131104 | tf_op jit(solution)/shard_map/while/body/eval_jaxpr/ppermute | solution.py:13
  174.8 6.7 %collective-permute-done = bf16[2,256,1,128]{3,1,2,0:T(8,128)(2,1)S(1)} collective-permute-done((bf16[2,256,1,128]{3,1,2,0:T(8,128)(2,1)S(1)}, bf16[2,256,1,128]{3,1,2,0:T(8,128)(2,1)S(1)}, u32[]{:S(2)}, u32[]{:S(2)}) %collective-permute-start) | collective-permute-done | bytes 131104 | tf_op jit(solution)/shard_map/while/body/eval_jaxpr/ppermute | solution.py:13
  185.7 6.7 %collective-permute-done = bf16[2,256,1,128]{3,1,2,0:T(8,128)(2,1)S(1)} collective-permute-done((bf16[2,256,1,128]{3,1,2,0:T(8,128)(2,1)S(1)}, bf16[2,256,1,128]{3,1,2,0:T(8,128)(2,1)S(1)}, u32[]{:S(2)}, u32[]{:S(2)}) %collective-permute-start) | collective-permute-done | bytes 131104 | tf_op jit(solution)/shard_map/while/body/eval_jaxpr/ppermute | solution.py:13
  196.7 6.7 %collective-permute-done = bf16[2,256,1,128]{3,1,2,0:T(8,128)(2,1)S(1)} collective-permute-done((bf16[2,256,1,128]{3,1,2,0:T(8,128)(2,1)S(1)}, bf16[2,256,1,128]{3,1,2,0:T(8,128)(2,1)S(1)}, u32[]{:S(2)}, u32[]{:S(2)}) %collective-permute-start) | collective-permute-done | bytes 131104 | tf_op jit(solution)/shard_map/while/body/eval_jaxpr/ppermute | solution.py:13
  207.6 6.7 %collective-permute-done = bf16[2,256,1,128]{3,1,2,0:T(8,128)(2,1)S(1)} collective-permute-done((bf16[2,256,1,128]{3,1,2,0:T(8,128)(2,1)S(1)}, bf16[2,256,1,128]{3,1,2,0:T(8,128)(2,1)S(1)}, u32[]{:S(2)}, u32[]{:S(2)}) %collective-permute-start) | collective-permute-done | bytes 131104 | tf_op jit(solution)/shard_map/while/body/eval_jaxpr/ppermute | solution.py:13
  229.5 6.7 %collective-permute-done = bf16[2,256,1,128]{3,1,2,0:T(8,128)(2,1)S(1)} collective-permute-done((bf16[2,256,1,128]{3,1,2,0:T(8,128)(2,1)S(1)}, bf16[2,256,1,128]{3,1,2,0:T(8,128)(2,1)S(1)}, u32[]{:S(2)}, u32[]{:S(2)}) %collective-permute-start) | collective-permute-done | bytes 131104 | tf_op jit(solution)/shard_map/while/body/eval_jaxpr/ppermute | solution.py:13
  240.5 6.7 %collective-permute-done = bf16[2,256,1,128]{3,1,2,0:T(8,128)(2,1)S(1)} collective-permute-done((bf16[2,256,1,128]{3,1,2,0:T(8,128)(2,1)S(1)}, bf16[2,256,1,128]{3,1,2,0:T(8,128)(2,1)S(1)}, u32[]{:S(2)}, u32[]{:S(2)}) %collective-permute-start) | collective-permute-done | bytes 131104 | tf_op jit(solution)/shard_map/while/body/eval_jaxpr/ppermute | solution.py:13
  251.4 6.7 %collective-permute-done = bf16[2,256,1,128]{3,1,2,0:T(8,128)(2,1)S(1)} collective-permute-done((bf16[2,256,1,128]{3,1,2,0:T(8,128)(2,1)S(1)}, bf16[2,256,1,128]{3,1,2,0:T(8,128)(2,1)S(1)}, u32[]{:S(2)}, u32[]{:S(2)}) %collective-permute-start) | collective-permute-done | bytes 131104 | tf_op jit(solution)/shard_map/while/body/eval_jaxpr/ppermute | solution.py:13
  262.4 6.7 %collective-permute-done = bf16[2,256,1,128]{3,1,2,0:T(8,128)(2,1)S(1)} collective-permute-done((bf16[2,256,1,128]{3,1,2,0:T(8,128)(2,1)S(1)}, bf16[2,256,1,128]{3,1,2,0:T(8,128)(2,1)S(1)}, u32[]{:S(2)}, u32[]{:S(2)}) %collective-permute-start) | collective-permute-done | bytes 131104 | tf_op jit(solution)/shard_map/while/body/eval_jaxpr/ppermute | solution.py:13
  273.3 6.7 %collective-permute-done = bf16[2,256,1,128]{3,1,2,0:T(8,128)(2,1)S(1)} collective-permute-done((bf16[2,256,1,128]{3,1,2,0:T(8,128)(2,1)S(1)}, bf16[2,256,1,128]{3,1,2,0:T(8,128)(2,1)S(1)}, u32[]{:S(2)}, u32[]{:S(2)}) %collective-permute-start) | collective-permute-done | bytes 131104 | tf_op jit(solution)/shard_map/while/body/eval_jaxpr/ppermute | solution.py:13
  284.3 6.7 %collective-permute-done = bf16[2,256,1,128]{3,1,2,0:T(8,128)(2,1)S(1)} collective-permute-done((bf16[2,256,1,128]{3,1,2,0:T(8,128)(2,1)S(1)}, bf16[2,256,1,128]{3,1,2,0:T(8,128)(2,1)S(1)}, u32[]{:S(2)}, u32[]{:S(2)}) %collective-permute-start) | collective-permute-done | bytes 131104 | tf_op jit(solution)/shard_map/while/body/eval_jaxpr/ppermute | solution.py:13
  306.2 6.7 %collective-permute-done = bf16[2,256,1,128]{3,1,2,0:T(8,128)(2,1)S(1)} collective-permute-done((bf16[2,256,1,128]{3,1,2,0:T(8,128)(2,1)S(1)}, bf16[2,256,1,128]{3,1,2,0:T(8,128)(2,1)S(1)}, u32[]{:S(2)}, u32[]{:S(2)}) %collective-permute-start) | collective-permute-done | bytes 131104 | tf_op jit(solution)/shard_map/while/body/eval_jaxpr/ppermute | solution.py:13
  317.1 6.7 %collective-permute-done = bf16[2,256,1,128]{3,1,2,0:T(8,128)(2,1)S(1)} collective-permute-done((bf16[2,256,1,128]{3,1,2,0:T(8,128)(2,1)S(1)}, bf16[2,256,1,128]{3,1,2,0:T(8,128)(2,1)S(1)}, u32[]{:S(2)}, u32[]{:S(2)}) %collective-permute-start) | collective-permute-done | bytes 131104 | tf_op jit(solution)/shard_map/while/body/eval_jaxpr/ppermute | solution.py:13
  328.0 6.7 %collective-permute-done = bf16[2,256,1,128]{3,1,2,0:T(8,128)(2,1)S(1)} collective-permute-done((bf16[2,256,1,128]{3,1,2,0:T(8,128)(2,1)S(1)}, bf16[2,256,1,128]{3,1,2,0:T(8,128)(2,1)S(1)}, u32[]{:S(2)}, u32[]{:S(2)}) %collective-permute-start) | collective-permute-done | bytes 131104 | tf_op jit(solution)/shard_map/while/body/eval_jaxpr/ppermute | solution.py:13
  339.0 6.7 %collective-permute-done = bf16[2,256,1,128]{3,1,2,0:T(8,128)(2,1)S(1)} collective-permute-done((bf16[2,256,1,128]{3,1,2,0:T(8,128)(2,1)S(1)}, bf16[2,256,1,128]{3,1,2,0:T(8,128)(2,1)S(1)}, u32[]{:S(2)}, u32[]{:S(2)}) %collective-permute-start) | collective-permute-done | bytes 131104 | tf_op jit(solution)/shard_map/while/body/eval_jaxpr/ppermute | solution.py:13
  406.0 49.9 %all-gather.5.cloned.1.call-done = bf16[8192,256]{1,0:T(8,128)(2,1)} async-done(((bf16[256,256]{1,0:T(8,128)(2,1)}), bf16[8192,256]{1,0:T(8,128)(2,1)}) %all-gather.5.cloned.1.call-update) | async-done | bytes 4194320 | tf_op jit(solution)/shard_map/all_gather | solution.py:131
  (491 shorter events, 216.1 us)
Async XLA Ops:
  7.2 43.9 %all-gather.3.cloned.1.call-start = ((), (), s32[]{:S(2)}) async-start(), calls=%async_computation | async-start | bytes 2359296 | tf_op jit(solution)/shard_map/all_gather | solution.py:92
  7.9 448.1 %all-gather.5.cloned.1.call-start = ((), (), s32[]{:S(2)}) async-start(), calls=%async_computation.1 | async-start | bytes 4325376 | tf_op jit(solution)/shard_map/all_gather | solution.py:131
  86.6 9.2 %collective-permute-start.1 = (f32[2,256,1,128]{3,1,2,0:T(8,128)S(1)}, f32[2,256,1,128]{3,1,2,0:T(8,128)S(1)}, u32[]{:S(2)}, u32[]{:S(2)}) collective-permute-start(f32[2,256,1,128]{3,1,2,0:T(8,128)S(1)} %maximum_add_fusion.2), channel_id=1, source_target_pairs={{0,8},{8,16},{16,24},{24,32},{32,40},{40,48},{48,56},{56,64},{64,7... | collective-permute-start | bytes 786440 | tf_op jit(solution)/shard_map/while/body/eval_jaxpr/ppermute | solution.py:13
  97.6 9.2 %collective-permute-start.1 = (f32[2,256,1,128]{3,1,2,0:T(8,128)S(1)}, f32[2,256,1,128]{3,1,2,0:T(8,128)S(1)}, u32[]{:S(2)}, u32[]{:S(2)}) collective-permute-start(f32[2,256,1,128]{3,1,2,0:T(8,128)S(1)} %maximum_add_fusion.2), channel_id=1, source_target_pairs={{0,8},{8,16},{16,24},{24,32},{32,40},{40,48},{48,56},{56,64},{64,7... | collective-permute-start | bytes 786440 | tf_op jit(solution)/shard_map/while/body/eval_jaxpr/ppermute | solution.py:13
  108.5 9.2 %collective-permute-start.1 = (f32[2,256,1,128]{3,1,2,0:T(8,128)S(1)}, f32[2,256,1,128]{3,1,2,0:T(8,128)S(1)}, u32[]{:S(2)}, u32[]{:S(2)}) collective-permute-start(f32[2,256,1,128]{3,1,2,0:T(8,128)S(1)} %maximum_add_fusion.2), channel_id=1, source_target_pairs={{0,8},{8,16},{16,24},{24,32},{32,40},{40,48},{48,56},{56,64},{64,7... | collective-permute-start | bytes 786440 | tf_op jit(solution)/shard_map/while/body/eval_jaxpr/ppermute | solution.py:13
  119.5 9.2 %collective-permute-start.1 = (f32[2,256,1,128]{3,1,2,0:T(8,128)S(1)}, f32[2,256,1,128]{3,1,2,0:T(8,128)S(1)}, u32[]{:S(2)}, u32[]{:S(2)}) collective-permute-start(f32[2,256,1,128]{3,1,2,0:T(8,128)S(1)} %maximum_add_fusion.2), channel_id=1, source_target_pairs={{0,8},{8,16},{16,24},{24,32},{32,40},{40,48},{48,56},{56,64},{64,7... | collective-permute-start | bytes 786440 | tf_op jit(solution)/shard_map/while/body/eval_jaxpr/ppermute | solution.py:13
  130.4 9.2 %collective-permute-start.1 = (f32[2,256,1,128]{3,1,2,0:T(8,128)S(1)}, f32[2,256,1,128]{3,1,2,0:T(8,128)S(1)}, u32[]{:S(2)}, u32[]{:S(2)}) collective-permute-start(f32[2,256,1,128]{3,1,2,0:T(8,128)S(1)} %maximum_add_fusion.2), channel_id=1, source_target_pairs={{0,8},{8,16},{16,24},{24,32},{32,40},{40,48},{48,56},{56,64},{64,7... | collective-permute-start | bytes 786440 | tf_op jit(solution)/shard_map/while/body/eval_jaxpr/ppermute | solution.py:13
  141.4 9.2 %collective-permute-start.1 = (f32[2,256,1,128]{3,1,2,0:T(8,128)S(1)}, f32[2,256,1,128]{3,1,2,0:T(8,128)S(1)}, u32[]{:S(2)}, u32[]{:S(2)}) collective-permute-start(f32[2,256,1,128]{3,1,2,0:T(8,128)S(1)} %maximum_add_fusion.2), channel_id=1, source_target_pairs={{0,8},{8,16},{16,24},{24,32},{32,40},{40,48},{48,56},{56,64},{64,7... | collective-permute-start | bytes 786440 | tf_op jit(solution)/shard_map/while/body/eval_jaxpr/ppermute | solution.py:13
  152.3 9.2 %collective-permute-start.1 = (f32[2,256,1,128]{3,1,2,0:T(8,128)S(1)}, f32[2,256,1,128]{3,1,2,0:T(8,128)S(1)}, u32[]{:S(2)}, u32[]{:S(2)}) collective-permute-start(f32[2,256,1,128]{3,1,2,0:T(8,128)S(1)} %maximum_add_fusion.2), channel_id=1, source_target_pairs={{0,8},{8,16},{16,24},{24,32},{32,40},{40,48},{48,56},{56,64},{64,7... | collective-permute-start | bytes 786440 | tf_op jit(solution)/shard_map/while/body/eval_jaxpr/ppermute | solution.py:13
  163.3 9.2 %collective-permute-start.1 = (f32[2,256,1,128]{3,1,2,0:T(8,128)S(1)}, f32[2,256,1,128]{3,1,2,0:T(8,128)S(1)}, u32[]{:S(2)}, u32[]{:S(2)}) collective-permute-start(f32[2,256,1,128]{3,1,2,0:T(8,128)S(1)} %maximum_add_fusion.2), channel_id=1, source_target_pairs={{0,8},{8,16},{16,24},{24,32},{32,40},{40,48},{48,56},{56,64},{64,7... | collective-permute-start | bytes 786440 | tf_op jit(solution)/shard_map/while/body/eval_jaxpr/ppermute | solution.py:13
  174.2 9.2 %collective-permute-start.1 = (f32[2,256,1,128]{3,1,2,0:T(8,128)S(1)}, f32[2,256,1,128]{3,1,2,0:T(8,128)S(1)}, u32[]{:S(2)}, u32[]{:S(2)}) collective-permute-start(f32[2,256,1,128]{3,1,2,0:T(8,128)S(1)} %maximum_add_fusion.2), channel_id=1, source_target_pairs={{0,8},{8,16},{16,24},{24,32},{32,40},{40,48},{48,56},{56,64},{64,7... | collective-permute-start | bytes 786440 | tf_op jit(solution)/shard_map/while/body/eval_jaxpr/ppermute | solution.py:13
  185.2 9.2 %collective-permute-start.1 = (f32[2,256,1,128]{3,1,2,0:T(8,128)S(1)}, f32[2,256,1,128]{3,1,2,0:T(8,128)S(1)}, u32[]{:S(2)}, u32[]{:S(2)}) collective-permute-start(f32[2,256,1,128]{3,1,2,0:T(8,128)S(1)} %maximum_add_fusion.2), channel_id=1, source_target_pairs={{0,8},{8,16},{16,24},{24,32},{32,40},{40,48},{48,56},{56,64},{64,7... | collective-permute-start | bytes 786440 | tf_op jit(solution)/shard_map/while/body/eval_jaxpr/ppermute | solution.py:13
  196.1 9.2 %collective-permute-start.1 = (f32[2,256,1,128]{3,1,2,0:T(8,128)S(1)}, f32[2,256,1,128]{3,1,2,0:T(8,128)S(1)}, u32[]{:S(2)}, u32[]{:S(2)}) collective-permute-start(f32[2,256,1,128]{3,1,2,0:T(8,128)S(1)} %maximum_add_fusion.2), channel_id=1, source_target_pairs={{0,8},{8,16},{16,24},{24,32},{32,40},{40,48},{48,56},{56,64},{64,7... | collective-permute-start | bytes 786440 | tf_op jit(solution)/shard_map/while/body/eval_jaxpr/ppermute | solution.py:13
  207.1 9.2 %collective-permute-start.1 = (f32[2,256,1,128]{3,1,2,0:T(8,128)S(1)}, f32[2,256,1,128]{3,1,2,0:T(8,128)S(1)}, u32[]{:S(2)}, u32[]{:S(2)}) collective-permute-start(f32[2,256,1,128]{3,1,2,0:T(8,128)S(1)} %maximum_add_fusion.2), channel_id=1, source_target_pairs={{0,8},{8,16},{16,24},{24,32},{32,40},{40,48},{48,56},{56,64},{64,7... | collective-permute-start | bytes 786440 | tf_op jit(solution)/shard_map/while/body/eval_jaxpr/ppermute | solution.py:13
  218.0 9.2 %collective-permute-start.1 = (f32[2,256,1,128]{3,1,2,0:T(8,128)S(1)}, f32[2,256,1,128]{3,1,2,0:T(8,128)S(1)}, u32[]{:S(2)}, u32[]{:S(2)}) collective-permute-start(f32[2,256,1,128]{3,1,2,0:T(8,128)S(1)} %maximum_add_fusion.2), channel_id=1, source_target_pairs={{0,8},{8,16},{16,24},{24,32},{32,40},{40,48},{48,56},{56,64},{64,7... | collective-permute-start | bytes 786440 | tf_op jit(solution)/shard_map/while/body/eval_jaxpr/ppermute | solution.py:13
  229.0 9.2 %collective-permute-start.1 = (f32[2,256,1,128]{3,1,2,0:T(8,128)S(1)}, f32[2,256,1,128]{3,1,2,0:T(8,128)S(1)}, u32[]{:S(2)}, u32[]{:S(2)}) collective-permute-start(f32[2,256,1,128]{3,1,2,0:T(8,128)S(1)} %maximum_add_fusion.2), channel_id=1, source_target_pairs={{0,8},{8,16},{16,24},{24,32},{32,40},{40,48},{48,56},{56,64},{64,7... | collective-permute-start | bytes 786440 | tf_op jit(solution)/shard_map/while/body/eval_jaxpr/ppermute | solution.py:13
  239.9 9.2 %collective-permute-start.1 = (f32[2,256,1,128]{3,1,2,0:T(8,128)S(1)}, f32[2,256,1,128]{3,1,2,0:T(8,128)S(1)}, u32[]{:S(2)}, u32[]{:S(2)}) collective-permute-start(f32[2,256,1,128]{3,1,2,0:T(8,128)S(1)} %maximum_add_fusion.2), channel_id=1, source_target_pairs={{0,8},{8,16},{16,24},{24,32},{32,40},{40,48},{48,56},{56,64},{64,7... | collective-permute-start | bytes 786440 | tf_op jit(solution)/shard_map/while/body/eval_jaxpr/ppermute | solution.py:13
  250.9 9.2 %collective-permute-start.1 = (f32[2,256,1,128]{3,1,2,0:T(8,128)S(1)}, f32[2,256,1,128]{3,1,2,0:T(8,128)S(1)}, u32[]{:S(2)}, u32[]{:S(2)}) collective-permute-start(f32[2,256,1,128]{3,1,2,0:T(8,128)S(1)} %maximum_add_fusion.2), channel_id=1, source_target_pairs={{0,8},{8,16},{16,24},{24,32},{32,40},{40,48},{48,56},{56,64},{64,7... | collective-permute-start | bytes 786440 | tf_op jit(solution)/shard_map/while/body/eval_jaxpr/ppermute | solution.py:13
  261.8 9.2 %collective-permute-start.1 = (f32[2,256,1,128]{3,1,2,0:T(8,128)S(1)}, f32[2,256,1,128]{3,1,2,0:T(8,128)S(1)}, u32[]{:S(2)}, u32[]{:S(2)}) collective-permute-start(f32[2,256,1,128]{3,1,2,0:T(8,128)S(1)} %maximum_add_fusion.2), channel_id=1, source_target_pairs={{0,8},{8,16},{16,24},{24,32},{32,40},{40,48},{48,56},{56,64},{64,7... | collective-permute-start | bytes 786440 | tf_op jit(solution)/shard_map/while/body/eval_jaxpr/ppermute | solution.py:13
  272.8 9.2 %collective-permute-start.1 = (f32[2,256,1,128]{3,1,2,0:T(8,128)S(1)}, f32[2,256,1,128]{3,1,2,0:T(8,128)S(1)}, u32[]{:S(2)}, u32[]{:S(2)}) collective-permute-start(f32[2,256,1,128]{3,1,2,0:T(8,128)S(1)} %maximum_add_fusion.2), channel_id=1, source_target_pairs={{0,8},{8,16},{16,24},{24,32},{32,40},{40,48},{48,56},{56,64},{64,7... | collective-permute-start | bytes 786440 | tf_op jit(solution)/shard_map/while/body/eval_jaxpr/ppermute | solution.py:13
  283.7 9.2 %collective-permute-start.1 = (f32[2,256,1,128]{3,1,2,0:T(8,128)S(1)}, f32[2,256,1,128]{3,1,2,0:T(8,128)S(1)}, u32[]{:S(2)}, u32[]{:S(2)}) collective-permute-start(f32[2,256,1,128]{3,1,2,0:T(8,128)S(1)} %maximum_add_fusion.2), channel_id=1, source_target_pairs={{0,8},{8,16},{16,24},{24,32},{32,40},{40,48},{48,56},{56,64},{64,7... | collective-permute-start | bytes 786440 | tf_op jit(solution)/shard_map/while/body/eval_jaxpr/ppermute | solution.py:13
  305.6 9.2 %collective-permute-start.1 = (f32[2,256,1,128]{3,1,2,0:T(8,128)S(1)}, f32[2,256,1,128]{3,1,2,0:T(8,128)S(1)}, u32[]{:S(2)}, u32[]{:S(2)}) collective-permute-start(f32[2,256,1,128]{3,1,2,0:T(8,128)S(1)} %maximum_add_fusion.2), channel_id=1, source_target_pairs={{0,8},{8,16},{16,24},{24,32},{32,40},{40,48},{48,56},{56,64},{64,7... | collective-permute-start | bytes 786440 | tf_op jit(solution)/shard_map/while/body/eval_jaxpr/ppermute | solution.py:13
  360.3 9.2 %collective-permute-start.1 = (f32[2,256,1,128]{3,1,2,0:T(8,128)S(1)}, f32[2,256,1,128]{3,1,2,0:T(8,128)S(1)}, u32[]{:S(2)}, u32[]{:S(2)}) collective-permute-start(f32[2,256,1,128]{3,1,2,0:T(8,128)S(1)} %maximum_add_fusion.2), channel_id=1, source_target_pairs={{0,8},{8,16},{16,24},{24,32},{32,40},{40,48},{48,56},{56,64},{64,7... | collective-permute-start | bytes 786440 | tf_op jit(solution)/shard_map/while/body/eval_jaxpr/ppermute | solution.py:13
  382.2 9.2 %collective-permute-start.1 = (f32[2,256,1,128]{3,1,2,0:T(8,128)S(1)}, f32[2,256,1,128]{3,1,2,0:T(8,128)S(1)}, u32[]{:S(2)}, u32[]{:S(2)}) collective-permute-start(f32[2,256,1,128]{3,1,2,0:T(8,128)S(1)} %maximum_add_fusion.2), channel_id=1, source_target_pairs={{0,8},{8,16},{16,24},{24,32},{32,40},{40,48},{48,56},{56,64},{64,7... | collective-permute-start | bytes 786440 | tf_op jit(solution)/shard_map/while/body/eval_jaxpr/ppermute | solution.py:13
  (44 other events, 752.3 us)
Sparse Core Ops, SparseCore 0:
  9.8 41.2 all-gather.2
  403.2 52.7 all-gather.4
where the time goes:
time: 465 us; the launch traced here: 464 us
  waiting for transfers between devices  352 us (76%)
  matrix products  59.3 us (13%)
  starting transfers between devices  15.9 us (3%)
  between operations  15.5 us (3%)
  other arithmetic  13.9 us (3%)
  local copies, waits for them, and re-layouts  5.1 us (1%)
    ppermute x64, waiting for transfers between devices, shifted(): lax.ppermute(value, axis, [(i, (i + by) % peers) for i in range(peers)])  262 us
    all_gather x1, waiting for transfers between devices, per_device(): shards = lax.all_gather(finished, 'seq', axis=0, tiled=True)  49.9 us
    all_gather x1, waiting for transfers between devices, per_device(): lax.all_gather(upstream, 'head', axis=1, tiled=True)  38.9 us
    ppermute x64, starting transfers between devices, shifted(): lax.ppermute(value, axis, [(i, (i + by) % peers) for i in range(peers)])  15.8 us
    dot_general x32, matrix products, grad_tile(): jnp.einsum('cgqk,kcd->qcgd', score_grad, key_rows, preferred_element_type...  14.6 us
    dot_general x32, matrix products, tile_scores(): jnp.einsum('qcgd,kcd->cgqk', queries, key_rows, preferred_element_type=jn...  12.1 us
    dot_general x32, matrix products, grad_tile(): jnp.einsum('qcgd,kcd->cgqk', out_grad, value_rows, preferred_element_type...  9.68 us
    dot_general x32, matrix products, grad_tile(): jnp.einsum('cgqk,qcgd->kcd', score_grad, queries, preferred_element_type=...  9.52 us
  transfers between devices with their start and end apart: 66, of which 65 were waited for; matrix products, arithmetic and copies ran while one was open for 15% of the time, Pallas kernels for 0%

commit v1 on v0

v1 whole, which is shorter than its diff:
```python
import functools
import math

import jax
import jax.numpy as jnp
from jax import lax
from jax.experimental import pallas as pl
from jax.experimental.pallas import tpu as pltpu
from jax.sharding import PartitionSpec as P

HD = 128
GROUP = 4
SIDE = 4
CHIPS = SIDE * SIDE
HEADS = 8
BLOCKS = 64
MINE = BLOCKS // 2
STACK = GROUP * HD
FACTOR = 1.0 / math.sqrt(HD)
LOG2E = math.log2(math.e)
VMEM_BYTES = 48 * 1024 * 1024

NT = (((1,), (1,)), ((), ()))
TN = (((0,), (0,)), ((), ()))
NN = (((1,), (0,)), ((), ()))

SWAP = [(i, i ^ 1) for i in range(2 * CHIPS)]
SAME_CORE = [[2 * c + k for c in range(CHIPS)] for k in range(2)]


def chip_shift(dx, dy):
    pairs = []
    for x in range(SIDE):
        for y in range(SIDE):
            target = ((x + dx) % SIDE) * SIDE + (y + dy) % SIDE
            for core in range(2):
                pairs.append(((x * SIDE + y) * 2 + core, target * 2 + core))
    return pairs


def head_shift(by):
    return [(i, (i + by) % HEADS) for i in range(HEADS)]


def swapped(value):
    return lax.ppermute(value, "seq", SWAP)


def vmem():
    return pl.BlockSpec(memory_space=pltpu.VMEM)


def smem():
    return pl.BlockSpec(memory_space=pltpu.SMEM)


def project_first(u0, u1, u2, u3, u4, w0, w1, w2, w3, w4, total_ref):
    total = lax.dot_general(u0[...], w0[...], NT, preferred_element_type=jnp.float32)
    for u, w in ((u1, w1), (u2, w2), (u3, w3), (u4, w4)):
        total += lax.dot_general(u[...], w[...], NT, preferred_element_type=jnp.float32)
    total_ref[...] = total


def project_last(total_ref, u5, u6, top, bottom, w5, w6, w7, attention_ref, grad_ref, delta_ref):
    for slot, far in ((0, top), (1, bottom)):
        rows = slice(slot * HD, (slot + 1) * HD)
        total = total_ref[rows, :]
        total += lax.dot_general(u5[rows, :], w5[...], NT, preferred_element_type=jnp.float32)
        total += lax.dot_general(u6[rows, :], w6[...], NT, preferred_element_type=jnp.float32)
        total += lax.dot_general(far[...], w7[...], NT, preferred_element_type=jnp.float32)
        grad = total.astype(jnp.bfloat16)
        products = grad.astype(jnp.float32) * attention_ref[rows, :].astype(jnp.float32)
        for g in range(GROUP):
            columns = slice(g * HD, (g + 1) * HD)
            grad_ref[slot * STACK + g * HD : slot * STACK + (g + 1) * HD, :] = grad[:, columns]
            delta_ref[slot, :, columns] = jnp.sum(
                jnp.transpose(products[:, columns]), axis=0, keepdims=True
            )


def sort_keys(source_ref, keys_ref, values_ref, sorted_keys, sorted_values):
    def move(n, carry):
        source = pl.multiple_of(source_ref[0, n] * HD, HD)
        target = pl.multiple_of(n * HD, HD)
        sorted_keys[pl.ds(target, HD), :] = keys_ref[pl.ds(source, HD), :]
        source = pl.multiple_of(source_ref[1, n] * HD, HD)
        sorted_values[pl.ds(target, HD), :] = values_ref[pl.ds(source, HD), :]
        return carry

    lax.fori_loop(0, MINE, move, 0)
    sorted_keys[MINE * HD :, :] = jnp.zeros((HD, HD), jnp.bfloat16)
    sorted_values[MINE * HD :, :] = jnp.zeros((HD, HD), jnp.bfloat16)


def attend(
    position_ref,
    slot_ref,
    bound_ref,
    keys_ref,
    values_ref,
    q_own,
    q_sib,
    do_own,
    do_sib,
    norm_ref,
    first_ref,
    last_ref,
    delta_own,
    delta_sib,
    parts_ref,
    dq_own,
    dq_sib,
    dk_ref,
    dv_ref,
    dqt_ref,
):
    dk_ref[...] = jnp.zeros_like(dk_ref)
    dv_ref[...] = jnp.zeros_like(dv_ref)
    upper = lax.broadcasted_iota(jnp.int32, (2 * HD, 1), 0)
    for block in range(4):
        q_ref, do_ref, delta_ref, dq_ref = (
            (q_own, do_own, delta_own, dq_own),
            (q_sib, do_sib, delta_sib, dq_sib),
        )[block // 2]
        slot = block % 2
        rows = slice(slot * STACK, (slot + 1) * STACK)
        norm = norm_ref[block]
        first = first_ref[block]
        last = last_ref[block]
        delta = delta_ref[slot]
        begin = bound_ref[2 * block]
        end = bound_ref[2 * block + 1]
        dqt_ref[...] = jnp.zeros_like(dqt_ref)

        def visit(step, carry):
            index = begin + 2 * step
            here = pl.ds(pl.multiple_of(index * HD, HD), 2 * HD)
            queries = q_ref[rows, :]
            grads = do_ref[rows, :]
            keys = keys_ref[here, :]
            scores = lax.dot_general(keys, queries, NT, preferred_element_type=jnp.float32)
            prob_grad = lax.dot_general(
                values_ref[here, :], grads, NT, preferred_element_type=jnp.float32
            )
            low = position_ref[index] * HD
            high = (position_ref[index + 1] - 1) * HD
            place = upper + jnp.where(upper < HD, low, high)
            allowed = (place >= first) & (place <= last)
            weights = jnp.where(allowed, jnp.exp2(scores * (FACTOR * LOG2E) - norm), 0.0)
            score_grad = (weights * (prob_grad - delta)).astype(jnp.bfloat16)
            dv_ref[here, :] += lax.dot_general(
                weights.astype(jnp.bfloat16), grads, NN, preferred_element_type=jnp.float32
            )
            dk_ref[here, :] += lax.dot_general(
                score_grad, queries, NN, preferred_element_type=jnp.float32
            )
            dqt_ref[...] += lax.dot_general(
                keys, score_grad, TN, preferred_element_type=jnp.float32
            )
            return carry

        lax.fori_loop(0, (end - begin + 1) // 2, visit, 0)
        for g in range(GROUP):
            columns = slice(g * HD, (g + 1) * HD)
            dq_ref[slot * HD : (slot + 1) * HD, columns] = (
                jnp.transpose(dqt_ref[:, columns]) * FACTOR
            )

    def hand_out(n, carry):
        source = pl.ds(pl.multiple_of(n * HD, HD), HD)
        target = pl.ds(pl.multiple_of(slot_ref[n] * HD, HD), HD)
        parts_ref[target, :HD] = (dk_ref[source, :] * FACTOR).astype(jnp.bfloat16)
        parts_ref[target, HD:] = dv_ref[source, :].astype(jnp.bfloat16)
        return carry

    lax.fori_loop(0, MINE, hand_out, 0)


def gather_chips(value, first, second):
    step = lambda axis, by: chip_shift(by, 0) if axis == "x" else chip_shift(0, by)
    near = [value] + [lax.ppermute(value, "seq", step(first, by)) for by in (1, 2, 3)]
    bundle = jnp.concatenate(near, axis=0)
    return [bundle] + [lax.ppermute(bundle, "seq", step(second, by)) for by in (1, 2, 3)]


def per_device(
    query_heads,
    key_heads,
    value_heads,
    attention_out,
    log_norm,
    upstream,
    output_weight,
    document_lengths,
    block_owners,
):
    me = lax.axis_index("seq")
    my_head = lax.axis_index("head")
    core = me % 2
    my_x = me // (2 * SIDE)
    my_y = (me // 2) % SIDE
    width = upstream.shape[1]

    forth, back = [upstream], [upstream]
    for _ in range(3):
        forth.append(lax.ppermute(forth[-1], "head", head_shift(1)))
        back.append(lax.ppermute(back[-1], "head", head_shift(-1)))
    top = lax.ppermute(forth[3][:HD], "head", head_shift(1))
    bottom = lax.ppermute(back[3][HD:], "head", head_shift(-1))

    def weight_of(offset):
        source = (my_head + offset) % HEADS
        return lax.dynamic_slice_in_dim(output_weight, source * width, width, 1)

    own_keys = gather_chips(key_heads, "y", "x")
    own_values = gather_chips(value_heads, "x", "y")
    keys_all = jnp.concatenate(own_keys + [swapped(v) for v in own_keys], axis=0)
    values_all = jnp.concatenate(own_values + [swapped(v) for v in own_values], axis=0)

    places = jnp.arange(BLOCKS, dtype=jnp.int32)
    row_block = jnp.where(places < MINE, 2 * places, 2 * (BLOCKS - 1 - places) + 1)
    target = jnp.sum(
        jnp.where(block_owners[None, :] == row_block[:, None], places[None, :], 0), axis=1
    )
    mine = (target // 2) % 2 == core
    rank = jnp.sum(
        (mine[None, :] & (places[None, :] < places[:, None])).astype(jnp.int32), axis=1
    )
    listed = mine[None, :] & (rank[None, :] == places[:MINE, None])

    def pick(values):
        return jnp.sum(jnp.where(listed, values[None, :], 0), axis=1)

    positions = pick(places)
    slots = pick((target // 4) * 2 + target % 2)
    chip = row_block // 4
    steps_x = (my_x - chip // SIDE) % SIDE
    steps_y = (my_y - chip % SIDE) % SIDE
    far_core = jnp.where((row_block // 2) % 2 == core, 0, MINE)
    sources = jnp.stack(
        [
            pick(far_core + (steps_x * SIDE + steps_y) * 2 + row_block % 2),
            pick(far_core + (steps_y * SIDE + steps_x) * 2 + row_block % 2),
        ]
    )
    sibling = me ^ 1
    query_blocks = jnp.stack([me, BLOCKS - 1 - me, sibling, BLOCKS - 1 - sibling])
    last = query_blocks[:, None] * HD + jnp.arange(HD, dtype=jnp.int32)[None, :]
    ends = jnp.cumsum(document_lengths)
    first = jnp.max(
        jnp.where(ends[None, None, :] <= last[:, :, None], ends[None, None, :], 0), axis=2
    )
    begin = jnp.sum((positions[None, :] < first[:, :1] // HD).astype(jnp.int32), axis=1)
    end = jnp.sum((positions[None, :] <= query_blocks[:, None]).astype(jnp.int32), axis=1)
    bounds = jnp.stack([begin, end], axis=1).reshape(8)
    padded = jnp.concatenate([positions, jnp.full((8,), 4 * BLOCKS, jnp.int32)])
    first = jnp.tile(first, (1, GROUP)).reshape(4, 1, STACK)
    last = jnp.tile(last, (1, GROUP)).reshape(4, 1, STACK)

    sorted_shape = jax.ShapeDtypeStruct(((MINE + 1) * HD, HD), jnp.bfloat16)
    keys, values = pl.pallas_call(
        sort_keys,
        out_shape=(sorted_shape, sorted_shape),
        in_specs=[smem(), vmem(), vmem()],
        out_specs=(vmem(), vmem()),
        compiler_params=pltpu.CompilerParams(vmem_limit_bytes=VMEM_BYTES),
        cost_estimate=pl.CostEstimate(flops=0, bytes_accessed=6 << 20, transcendentals=0),
        name="sort_keys",
    )(sources, keys_all, values_all)

    queries = (
        query_heads.reshape(2, HD, GROUP, HD).transpose(0, 2, 1, 3).reshape(2 * STACK, HD)
    )
    queries_sib = swapped(queries)
    norms = jnp.concatenate([log_norm, swapped(log_norm)], axis=1)
    norms = (norms * LOG2E).reshape(GROUP, 4, HD).transpose(1, 0, 2).reshape(4, 1, STACK)

    tokens = upstream.shape[0]
    total = pl.pallas_call(
        project_first,
        out_shape=jax.ShapeDtypeStruct((tokens, STACK), jnp.float32),
        in_specs=[vmem()] * 10,
        out_specs=vmem(),
        compiler_params=pltpu.CompilerParams(vmem_limit_bytes=VMEM_BYTES),
        cost_estimate=pl.CostEstimate(
            flops=2 * tokens * 5 * width * STACK, bytes_accessed=4 << 20, transcendentals=0
        ),
        name="project_first",
    )(
        upstream, forth[1], back[1], forth[2], back[2],
        *[weight_of(offset) for offset in (0, -1, 1, -2, 2)],
    )
    grads, delta = pl.pallas_call(
        project_last,
        out_shape=(
            jax.ShapeDtypeStruct((2 * STACK, HD), jnp.bfloat16),
            jax.ShapeDtypeStruct((2, 1, STACK), jnp.float32),
        ),
        in_specs=[vmem()] * 9,
        out_specs=(vmem(), vmem()),
        compiler_params=pltpu.CompilerParams(vmem_limit_bytes=VMEM_BYTES),
        cost_estimate=pl.CostEstimate(
            flops=2 * tokens * 3 * width * STACK, bytes_accessed=3 << 20, transcendentals=0
        ),
        name="project_last",
    )(
        total, forth[3], back[3], top, bottom,
        *[weight_of(offset) for offset in (-3, 3, 4)], attention_out,
    )
    grads_sib = swapped(grads)
    delta_sib = swapped(delta)

    parts, dq_own, dq_sib = pl.pallas_call(
        attend,
        out_shape=(
            jax.ShapeDtypeStruct((MINE * HD, 2 * HD), jnp.bfloat16),
            jax.ShapeDtypeStruct((tokens, STACK), jnp.float32),
            jax.ShapeDtypeStruct((tokens, STACK), jnp.float32),
        ),
        in_specs=[smem()] * 3 + [vmem()] * 11,
        out_specs=(vmem(), vmem(), vmem()),
        scratch_shapes=[
            pltpu.VMEM(((MINE + 1) * HD, HD), jnp.float32),
            pltpu.VMEM(((MINE + 1) * HD, HD), jnp.float32),
            pltpu.VMEM((HD, STACK), jnp.float32),
        ],
        compiler_params=pltpu.CompilerParams(vmem_limit_bytes=VMEM_BYTES),
        cost_estimate=pl.CostEstimate(
            flops=35 * 10 * GROUP * HD**3, bytes_accessed=8 << 20, transcendentals=0
        ),
        name="attend",
    )(
        padded, slots, bounds, keys, values, queries, queries_sib, grads, grads_sib,
        norms, first, last, delta, delta_sib,
    )
    query_grad = (dq_own + swapped(dq_sib)).astype(jnp.bfloat16)
    received = lax.all_to_all(
        parts.reshape(CHIPS, 2 * HD, 2 * HD), "seq", 0, 0, tiled=True,
        axis_index_groups=SAME_CORE,
    )
    finished = jnp.sum(received.astype(jnp.float32), axis=0).astype(jnp.bfloat16)
    return (query_grad, finished[:, :HD], finished[:, HD:])


def solution(mesh):
    placed = (
        P("seq", "head"),
        P("seq", "head"),
        P("seq", "head"),
        P("seq", "head"),
        P("head", "seq"),
        P("seq", "head"),
        P("head", None),
        P(),
        P(),
    )
    return jax.shard_map(
        per_device,
        mesh=mesh,
        in_specs=placed,
        out_specs=(P("seq", "head"), P("seq", "head"), P("seq", "head")),
        check_vma=False,
    )
```

time: 465 us -> 142 us (0.31)
  waiting for transfers between devices: 352 us -> 43.8 us
  matrix products: 59.3 us -> 0 us
  starting transfers between devices: 15.9 us -> 58.6 us
  local copies, waits for them, and re-layouts: 5.1 us -> 23.4 us
  between operations: 15.5 us -> 1.11 us
  Pallas kernels: 0 us -> 11.7 us
  other arithmetic: 13.9 us -> 4.44 us
    ppermute x64 -> x33, waiting for transfers between devices: 262 us -> 19.6 us  [the longest x6 14 us: gather_chips(): lax.ppermute(bundle, 'seq', step(second, by))]
    all_gather x2 -> x0, waiting for transfers between devices: 88.8 us -> none  [the longest x1 49.9 us: per_device(): shards = lax.all_gather(finished, 'seq', axis=0, tiled=True)]
    dot_general x161 -> x0, matrix products: 59.3 us -> none  [the longest x32 14.6 us: grad_tile(): jnp.einsum('cgqk,kcd->qcgd', score_grad, key_rows, preferred_element_type...]
    ppermute x64 -> x33, starting transfers between devices: 15.8 us -> 46.7 us  [the longest x13 17.3 us: swapped(): return lax.ppermute(value, 'seq', SWAP)]
    all_to_all x0 -> x1, waiting for transfers between devices: none -> 24.2 us  [per_device(): lax.all_to_all(parts.reshape(CHIPS, 2 * HD, 2 * HD), 'seq', 0, 0, tiled=T...]
    all_to_all x0 -> x1, starting transfers between devices: none -> 11.9 us  [per_device(): lax.all_to_all(parts.reshape(CHIPS, 2 * HD, 2 * HD), 'seq', 0, 0, tiled=T...]
    pallas_call x0 -> x4, Pallas kernels: none -> 11.7 us  [the longest x1 6.67 us: per_device(): pl.pallas_call(attend, out_shape=(jax.ShapeDtypeStruct((MINE * HD, 2 * HD...]
    unnamed x9 -> x50, local copies, waits for them, and re-layouts: 2.11 us -> 13.1 us
  transfers between devices with their start and end apart: 66 -> 34, of which waited for: 65 -> 5; matrix products, arithmetic and copies ran while one was open for 15% -> 18% of each run, Pallas kernels for 0% -> 4%
where the time goes in v1:
time: 142 us; the launch traced here: 143 us
  starting transfers between devices  58.6 us (41%)
  waiting for transfers between devices  43.8 us (31%)
  local copies, waits for them, and re-layouts  23.4 us (16%)
  Pallas kernels  11.7 us (8%)
  other arithmetic  4.44 us (3%)
    all_to_all x1, waiting for transfers between devices, per_device(): lax.all_to_all(parts.reshape(CHIPS, 2 * HD, 2 * HD), 'seq', 0, 0, tiled=T...  24.2 us
    ppermute x13, starting transfers between devices, swapped(): return lax.ppermute(value, 'seq', SWAP)  17.3 us
    ppermute x6, waiting for transfers between devices, gather_chips(): lax.ppermute(bundle, 'seq', step(second, by))  14 us
    unnamed x50, local copies, waits for them, and re-layouts  13.1 us
    all_to_all x1, starting transfers between devices, per_device(): lax.all_to_all(parts.reshape(CHIPS, 2 * HD, 2 * HD), 'seq', 0, 0, tiled=T...  11.9 us
    ppermute x6, starting transfers between devices, gather_chips(): lax.ppermute(value, 'seq', step(first, by))  9.96 us
    ppermute x3, starting transfers between devices, per_device(): back.append(lax.ppermute(back[-1], 'head', head_shift(-1)))  8.54 us
    pallas_call x1, Pallas kernels, per_device(): pl.pallas_call(attend, out_shape=(jax.ShapeDtypeStruct((MINE * HD, 2 * HD...  6.67 us
  transfers between devices with their start and end apart: 34, of which 5 were waited for; matrix products, arithmetic and copies ran while one was open for 18% of the time, Pallas kernels for 4%

profile of v1, /device:TPU:1, one launch (start us, length us, event | category | flops | bytes accessed | tf_op | source)
XLA Modules:
  0.0 143.0 jit_solution(16295347283920551947)
XLA Ops:
  0.6 2.5 %collective-permute-start.21 = (bf16[256,512]{1,0:T(8,128)(2,1)}, bf16[256,512]{1,0:T(8,128)(2,1)S(1)}, u32[]{:S(2)}, u32[]{:S(2)}) collective-permute-start(bf16[256,512]{1,0:T(8,128)(2,1)} %u0.1), channel_id=1, source_target_pairs={{0,1},{1,2},{2,3},{3,4},{4,5},{5,6},{6,7},{7,0},{8,9},{9,10},{10,1... | collective-permute-start | bytes 786440 | tf_op jit(solution)/shard_map/ppermute | solution.py:206
  3.2 4.0 %collective-permute-start.22 = (bf16[256,512]{1,0:T(8,128)(2,1)}, bf16[256,512]{1,0:T(8,128)(2,1)}, u32[]{:S(2)}, u32[]{:S(2)}) collective-permute-start(bf16[256,512]{1,0:T(8,128)(2,1)} %u0.1), channel_id=1, source_target_pairs={{0,7},{1,0},{2,1},{3,2},{4,3},{5,4},{6,5},{7,6},{8,15},{9,8},{10,9... | collective-permute-start | bytes 786440 | tf_op jit(solution)/shard_map/ppermute | solution.py:207
  8.4 2.5 %collective-permute-start.11 = (bf16[256,128]{1,0:T(8,128)(2,1)}, bf16[256,128]{1,0:T(8,128)(2,1)}, u32[]{:S(2)}, u32[]{:S(2)}) collective-permute-start(bf16[256,128]{1,0:T(8,128)(2,1)} %param.11), channel_id=1, source_target_pairs={{0,128},{8,136},{16,144},{24,152},{32,160},{40,168},{48,176},{56,1... | collective-permute-start | bytes 196616 | tf_op jit(solution)/shard_map/ppermute | solution.py:181
  10.9 1.5 %collective-permute-start.30 = (f32[4,256]{1,0:T(4,128)}, f32[4,256]{1,0:T(4,128)}, u32[]{:S(2)}, u32[]{:S(2)}) collective-permute-start(f32[4,256]{1,0:T(4,128)} %param.13), channel_id=1, source_target_pairs={{0,8},{8,0},{16,24},{24,16},{32,40},{40,32},{48,56},{56,48},{64,72... | collective-permute-start | bytes 12296 | tf_op jit(solution)/shard_map/ppermute | solution.py:46
  19.3 4.0 %constant_dynamic-slice_fusion = (bf16[512,512]{1,0:T(8,128)(2,1)}, bf16[512,512]{1,0:T(8,128)(2,1)}, bf16[512,512]{1,0:T(8,128)(2,1)S(1)}, bf16[512,512]{1,0:T(...) fusion(bf16[512,4096]{1,0:T(8,128)(2,1)} %param.15, ...), kind=kLoop, calls=%fused_computation.60 | loop fusion | bytes 8388640 | tf_op jit(solution)/shard_map/dynamic_slice | solution.py:213
  24.1 1.7 %reshape.326 = bf16[2,128,4,128]{3,2,1,0:T(4,128)(2,1)} reshape(bf16[256,512]{1,0:T(8,128)(2,1)} %param.9) | data formatting | bytes 524288 | tf_op jit(solution)/shard_map/reshape | solution.py:272
  31.7 2.6 %collective-permute-start.1 = (bf16[256,128]{1,0:T(8,128)(2,1)S(1)}, bf16[256,128]{1,0:T(8,128)(2,1)S(1)}, u32[]{:S(2)}, u32[]{:S(2)}) collective-permute-start(bf16[256,128]{1,0:T(8,128)(2,1)S(1)} %copy-done.9), channel_id=1, source_target_pairs={{0,32},{8,40},{16,48},{24,56},{32,0},{40,8},{48,16},{56,24},{64,96... | collective-permute-start | bytes 196616 | tf_op jit(solution)/shard_map/ppermute | solution.py:181
  34.3 1.5 %constant_dynamic-update-slice_fusion.16 = (bf16[1024,128]{1,0:T(8,128)(2,1)}, bf16[8192,128]{1,0:T(8,128)(2,1)}) fusion(bf16[1024,128]{1,0:T(8,128)(2,1)} %get-tuple-element.39, bf16[256,128]{1,0:T(8,128)(2,1)} %collective-permute-done.11, bf16[8192,128]{1,0:T(8,128)(2,1)} %get-tuple-element.40), kind=kLoop, calls=%fused_computation.17 | loop fusion | bytes 196608
  40.0 1.6 %collective-permute-start.15 = (bf16[1024,128]{1,0:T(8,128)(2,1)}, bf16[1024,128]{1,0:T(8,128)(2,1)S(1)}, u32[]{:S(2)}, u32[]{:S(2)}) collective-permute-start(bf16[1024,128]{1,0:T(8,128)(2,1)} %get-tuple-element.35), channel_id=1, source_target_pairs={{0,48},{8,56},{16,0},{24,8},{32,16},{40,24},{48,32},{56,40},{64,11... | collective-permute-start | bytes 786440 | tf_op jit(solution)/shard_map/ppermute | solution.py:183
  42.3 4.5 %collective-permute-done.13 = bf16[1024,128]{1,0:T(8,128)(2,1)S(1)} collective-permute-done((bf16[1024,128]{1,0:T(8,128)(2,1)}, bf16[1024,128]{1,0:T(8,128)(2,1)S(1)}, u32[]{:S(2)}, u32[]{:S(2)}) %collective-permute-start.13) | collective-permute-done | bytes 262176 | tf_op jit(solution)/shard_map/ppermute | solution.py:183
  46.8 6.5 %collective-permute-start.16 = (bf16[1024,128]{1,0:T(8,128)(2,1)}, bf16[1024,128]{1,0:T(8,128)(2,1)S(1)}, u32[]{:S(2)}, u32[]{:S(2)}) collective-permute-start(bf16[1024,128]{1,0:T(8,128)(2,1)} %get-tuple-element.35), channel_id=1, source_target_pairs={{0,8},{8,0},{16,24},{24,16},{32,40},{40,32},{48,56},{56,48},{64,72... | collective-permute-start | bytes 786440 | tf_op jit(solution)/shard_map/ppermute | solution.py:46
  59.5 9.5 %collective-permute-done.3 = bf16[1024,128]{1,0:T(8,128)(2,1)S(1)} collective-permute-done((bf16[1024,128]{1,0:T(8,128)(2,1)}, bf16[1024,128]{1,0:T(8,128)(2,1)S(1)}, u32[]{:S(2)}, u32[]{:S(2)}) %collective-permute-start.3) | collective-permute-done | bytes 262176 | tf_op jit(solution)/shard_map/ppermute | solution.py:183
  69.0 1.7 %collective-permute-start.24 = (bf16[256,512]{1,0:T(8,128)(2,1)}, bf16[256,512]{1,0:T(8,128)(2,1)S(1)}, u32[]{:S(2)}, u32[]{:S(2)}) collective-permute-start(bf16[256,512]{1,0:T(8,128)(2,1)} %collective-permute-done.22.u2), channel_id=1, source_target_pairs={{0,7},{1,0},{2,1},{3,2},{4,3},{5,4},{6,5},{7,6},{8,15},{9,8},{10,9... | collective-permute-start | bytes 786440 | tf_op jit(solution)/shard_map/ppermute | solution.py:207
  72.7 3.6 %collective-permute-done.24.u4 = bf16[256,512]{1,0:T(8,128)(2,1)S(1)} collective-permute-done((bf16[256,512]{1,0:T(8,128)(2,1)}, bf16[256,512]{1,0:T(8,128)(2,1)S(1)}, u32[]{:S(2)}, u32[]{:S(2)}) %collective-permute-start.24) | collective-permute-done | bytes 262176 | tf_op jit(solution)/shard_map/ppermute | solution.py:207
  76.3 2.9 %collective-permute-start.26 = (bf16[256,512]{1,0:T(8,128)(2,1)S(1)}, bf16[256,512]{1,0:T(8,128)(2,1)S(1)}, u32[]{:S(2)}, u32[]{:S(2)}) collective-permute-start(bf16[256,512]{1,0:T(8,128)(2,1)S(1)} %collective-permute-done.24.u4), channel_id=1, source_target_pairs={{0,7},{1,0},{2,1},{3,2},{4,3},{5,4},{6,5},{7,6},{8,15},{9,8},{10,9... | collective-permute-start | bytes 786440 | tf_op jit(solution)/shard_map/ppermute | solution.py:207
  79.2 1.8 %project_first.1.total_ref = f32[256,512]{1,0:T(8,128)S(1)} custom-call(bf16[256,512]{1,0:T(8,128)(2,1)S(1)} %copy-done.6, bf16[256,512]{1,0:T(8,128)(2,1)S(1)} %collective-permute-done.21.u1, bf16[256,512]{1,0:T(8,128)(2,1)} %collective-permute-done.22.u2, bf16[256,512]{1,0:T(8,128)(2,1)S(1)} %collective-permute-done.23.u3, ...), custom_call_target="tpu_custom_call" | custom-call | flops 671088640 | bytes 4194304 | tf_op jit(solution)/shard_map/project_first/pallas_call | solution.py:279
  81.1 2.1 %collective-permute-start.20 = (bf16[1024,128]{1,0:T(8,128)(2,1)S(1)}, bf16[1024,128]{1,0:T(8,128)(2,1)S(1)}, u32[]{:S(2)}, u32[]{:S(2)}) collective-permute-start(bf16[1024,128]{1,0:T(8,128)(2,1)S(1)} %bitcast.22), channel_id=1, source_target_pairs={{0,8},{8,0},{16,24},{24,16},{32,40},{40,32},{48,56},{56,48},{64,72... | collective-permute-start | bytes 786440 | tf_op jit(solution)/shard_map/ppermute | solution.py:46
  84.0 2.7 %collective-permute-start.28 = (bf16[128,512]{1,0:T(8,128)(2,1)S(1)}, bf16[128,512]{1,0:T(8,128)(2,1)S(1)}, u32[]{:S(2)}, u32[]{:S(2)}) collective-permute-start(bf16[128,512]{1,0:T(8,128)(2,1)S(1)} %slice.25), channel_id=1, source_target_pairs={{0,7},{1,0},{2,1},{3,2},{4,3},{5,4},{6,5},{7,6},{8,15},{9,8},{10,9... | collective-permute-start | bytes 393224 | tf_op jit(solution)/shard_map/ppermute | solution.py:209
  87.5 2.7 %collective-permute-start.8 = (bf16[1024,128]{1,0:T(8,128)(2,1)S(1)}, bf16[1024,128]{1,0:T(8,128)(2,1)S(1)}, u32[]{:S(2)}, u32[]{:S(2)}) collective-permute-start(bf16[1024,128]{1,0:T(8,128)(2,1)S(1)} %collective-permute-done.4), channel_id=1, source_target_pairs={{0,8},{8,0},{16,24},{24,16},{32,40},{40,32},{48,56},{56,48},{64,72... | collective-permute-start | bytes 786440 | tf_op jit(solution)/shard_map/ppermute | solution.py:46
  94.4 2.0 %sort_keys.1 = (bf16[4224,128]{1,0:T(8,128)(2,1)S(1)}, bf16[4224,128]{1,0:T(8,128)(2,1)S(1)}) custom-call(s32[2,32]{1,0:T(2,128)S(1)} %pad_add_fusion.1.source_ref, bf16[8192,128]{1,0:T(8,128)(2,1)S(1)} %constant_dynamic-update-slice_fusion.4.keys_ref, bf16[8192,128]{1,0:T(8,128)(2,1)} %constant_dynamic-update-slice_fusion.19.values_ref), custom_call_target="tpu_custom_call" | custom-call | bytes 6291456 | tf_op jit(solution)/shard_map/sort_keys/pallas_call | solution.py:261
  96.5 6.7 %attend.1 = (bf16[4096,256]{1,0:T(8,128)(2,1)}, f32[256,512]{1,0:T(8,128)S(1)}, f32[256,512]{1,0:T(8,128)S(1)}) custom-call(s32[40]{0:T(128)S(1)} %concatenate.29.position_ref, s32[32]{0:T(128)S(1)} %get-tuple-element.19.slot_ref, s32[8]{0:T(128)S(1)} %reshape.325.bound_ref, bf16[4224,128]{1,0:T(8,128)(2,1)S(1)} %get-tuple-element.10.keys_ref, ...), custom_call_target="tpu_custom_call" | custom-call | flops 2936012800 | bytes 8388608 | tf_op jit(solution)/shard_map/attend/pallas_call | solution.py:313
  103.1 11.9 %all-to-all-start = ((bf16[16,256,256]{2,1,0:T(8,128)(2,1)}), bf16[16,256,256]{2,1,0:T(8,128)(2,1)S(1)}, u32[]{:S(2)}, u32[]{:S(2)}) async-start(bf16[16,256,256]{2,1,0:T(8,128)(2,1)} %bitcast.27), calls=%async_computation | async-start | bytes 4194304 | tf_op jit(solution)/shard_map/all_to_all | solution.py:337
  115.1 1.9 %collective-permute-done.32 = f32[256,512]{1,0:T(8,128)S(1)} collective-permute-done((f32[256,512]{1,0:T(8,128)S(1)}, f32[256,512]{1,0:T(8,128)S(1)}, u32[]{:S(2)}, u32[]{:S(2)}) %collective-permute-start.32) | collective-permute-done | bytes 524320 | tf_op jit(solution)/shard_map/ppermute | solution.py:46
  117.8 24.2 %all-to-all-done = bf16[16,256,256]{2,1,0:T(8,128)(2,1)S(1)} async-done(((bf16[16,256,256]{2,1,0:T(8,128)(2,1)}), bf16[16,256,256]{2,1,0:T(8,128)(2,1)S(1)}, u32[]{:S(2)}, u32[]{:S(2)}) %all-to-all-start) | async-done | bytes 2097184 | tf_op jit(solution)/shard_map/all_to_all | solution.py:337
  (132 shorter events, 35.3 us)
Async XLA Ops:
  0.6 58.3 %collective-permute-start.21 = (bf16[256,512]{1,0:T(8,128)(2,1)}, bf16[256,512]{1,0:T(8,128)(2,1)S(1)}, u32[]{:S(2)}, u32[]{:S(2)}) collective-permute-start(bf16[256,512]{1,0:T(8,128)(2,1)} %u0.1), channel_id=1, source_target_pairs={{0,1},{1,2},{2,3},{3,4},{4,5},{5,6},{6,7},{7,0},{8,9},{9,10},{10,1... | collective-permute-start | bytes 786440 | tf_op jit(solution)/shard_map/ppermute | solution.py:206
  3.2 56.4 %collective-permute-start.22 = (bf16[256,512]{1,0:T(8,128)(2,1)}, bf16[256,512]{1,0:T(8,128)(2,1)}, u32[]{:S(2)}, u32[]{:S(2)}) collective-permute-start(bf16[256,512]{1,0:T(8,128)(2,1)} %u0.1), channel_id=1, source_target_pairs={{0,7},{1,0},{2,1},{3,2},{4,3},{5,4},{6,5},{7,6},{8,15},{9,8},{10,9... | collective-permute-start | bytes 786440 | tf_op jit(solution)/shard_map/ppermute | solution.py:207
  7.2 21.6 %collective-permute-start.10 = (bf16[256,128]{1,0:T(8,128)(2,1)}, bf16[256,128]{1,0:T(8,128)(2,1)}, u32[]{:S(2)}, u32[]{:S(2)}) collective-permute-start(bf16[256,128]{1,0:T(8,128)(2,1)} %param.11), channel_id=1, source_target_pairs={{0,64},{8,72},{16,80},{24,88},{32,96},{40,104},{48,112},{56,120},{... | collective-permute-start | bytes 196616 | tf_op jit(solution)/shard_map/ppermute | solution.py:181
  8.4 23.3 %collective-permute-start.11 = (bf16[256,128]{1,0:T(8,128)(2,1)}, bf16[256,128]{1,0:T(8,128)(2,1)}, u32[]{:S(2)}, u32[]{:S(2)}) collective-permute-start(bf16[256,128]{1,0:T(8,128)(2,1)} %param.11), channel_id=1, source_target_pairs={{0,128},{8,136},{16,144},{24,152},{32,160},{40,168},{48,176},{56,1... | collective-permute-start | bytes 196616 | tf_op jit(solution)/shard_map/ppermute | solution.py:181
  10.9 16.0 %collective-permute-start.30 = (f32[4,256]{1,0:T(4,128)}, f32[4,256]{1,0:T(4,128)}, u32[]{:S(2)}, u32[]{:S(2)}) collective-permute-start(f32[4,256]{1,0:T(4,128)} %param.13), channel_id=1, source_target_pairs={{0,8},{8,0},{16,24},{24,16},{32,40},{40,32},{48,56},{56,48},{64,72... | collective-permute-start | bytes 12296 | tf_op jit(solution)/shard_map/ppermute | solution.py:46
  26.9 9.0 %collective-permute-start.12 = (bf16[256,128]{1,0:T(8,128)(2,1)S(1)}, bf16[256,128]{1,0:T(8,128)(2,1)S(1)}, u32[]{:S(2)}, u32[]{:S(2)}) collective-permute-start(bf16[256,128]{1,0:T(8,128)(2,1)S(1)} %copy-done.8), channel_id=1, source_target_pairs={{0,192},{8,200},{16,208},{24,216},{32,224},{40,232},{48,240},{56,2... | collective-permute-start | bytes 196616 | tf_op jit(solution)/shard_map/ppermute | solution.py:181
  28.8 8.7 %collective-permute-start = (bf16[256,128]{1,0:T(8,128)(2,1)S(1)}, bf16[256,128]{1,0:T(8,128)(2,1)S(1)}, u32[]{:S(2)}, u32[]{:S(2)}) collective-permute-start(bf16[256,128]{1,0:T(8,128)(2,1)S(1)} %copy-done.9), channel_id=1, source_target_pairs={{0,16},{8,24},{16,32},{24,40},{32,48},{40,56},{48,0},{56,8},{64,80... | collective-permute-start | bytes 196616 | tf_op jit(solution)/shard_map/ppermute | solution.py:181
  37.5 9.3 %collective-permute-start.13 = (bf16[1024,128]{1,0:T(8,128)(2,1)}, bf16[1024,128]{1,0:T(8,128)(2,1)S(1)}, u32[]{:S(2)}, u32[]{:S(2)}) collective-permute-start(bf16[1024,128]{1,0:T(8,128)(2,1)} %get-tuple-element.35), channel_id=1, source_target_pairs={{0,16},{8,24},{16,32},{24,40},{32,48},{40,56},{48,0},{56,8},{64,80... | collective-permute-start | bytes 786440 | tf_op jit(solution)/shard_map/ppermute | solution.py:183
  38.6 15.5 %collective-permute-start.14 = (bf16[1024,128]{1,0:T(8,128)(2,1)}, bf16[1024,128]{1,0:T(8,128)(2,1)S(1)}, u32[]{:S(2)}, u32[]{:S(2)}) collective-permute-start(bf16[1024,128]{1,0:T(8,128)(2,1)} %get-tuple-element.35), channel_id=1, source_target_pairs={{0,32},{8,40},{16,48},{24,56},{32,0},{40,8},{48,16},{56,24},{64,96... | collective-permute-start | bytes 786440 | tf_op jit(solution)/shard_map/ppermute | solution.py:183
  40.0 15.1 %collective-permute-start.15 = (bf16[1024,128]{1,0:T(8,128)(2,1)}, bf16[1024,128]{1,0:T(8,128)(2,1)S(1)}, u32[]{:S(2)}, u32[]{:S(2)}) collective-permute-start(bf16[1024,128]{1,0:T(8,128)(2,1)} %get-tuple-element.35), channel_id=1, source_target_pairs={{0,48},{8,56},{16,0},{24,8},{32,16},{40,24},{48,32},{56,40},{64,11... | collective-permute-start | bytes 786440 | tf_op jit(solution)/shard_map/ppermute | solution.py:183
  46.8 9.9 %collective-permute-start.16 = (bf16[1024,128]{1,0:T(8,128)(2,1)}, bf16[1024,128]{1,0:T(8,128)(2,1)S(1)}, u32[]{:S(2)}, u32[]{:S(2)}) collective-permute-start(bf16[1024,128]{1,0:T(8,128)(2,1)} %get-tuple-element.35), channel_id=1, source_target_pairs={{0,8},{8,0},{16,24},{24,16},{32,40},{40,32},{48,56},{56,48},{64,72... | collective-permute-start | bytes 786440 | tf_op jit(solution)/shard_map/ppermute | solution.py:46
  54.0 15.0 %collective-permute-start.3 = (bf16[1024,128]{1,0:T(8,128)(2,1)}, bf16[1024,128]{1,0:T(8,128)(2,1)S(1)}, u32[]{:S(2)}, u32[]{:S(2)}) collective-permute-start(bf16[1024,128]{1,0:T(8,128)(2,1)} %get-tuple-element.43), channel_id=1, source_target_pairs={{0,64},{8,72},{16,80},{24,88},{32,96},{40,104},{48,112},{56,120},{... | collective-permute-start | bytes 786440 | tf_op jit(solution)/shard_map/ppermute | solution.py:183
  55.1 15.6 %collective-permute-start.4 = (bf16[1024,128]{1,0:T(8,128)(2,1)}, bf16[1024,128]{1,0:T(8,128)(2,1)S(1)}, u32[]{:S(2)}, u32[]{:S(2)}) collective-permute-start(bf16[1024,128]{1,0:T(8,128)(2,1)} %get-tuple-element.43), channel_id=1, source_target_pairs={{0,128},{8,136},{16,144},{24,152},{32,160},{40,168},{48,176},{56,1... | collective-permute-start | bytes 786440 | tf_op jit(solution)/shard_map/ppermute | solution.py:183
  56.7 15.2 %collective-permute-start.5 = (bf16[1024,128]{1,0:T(8,128)(2,1)}, bf16[1024,128]{1,0:T(8,128)(2,1)S(1)}, u32[]{:S(2)}, u32[]{:S(2)}) collective-permute-start(bf16[1024,128]{1,0:T(8,128)(2,1)} %get-tuple-element.43), channel_id=1, source_target_pairs={{0,192},{8,200},{16,208},{24,216},{32,224},{40,232},{48,240},{56,2... | collective-permute-start | bytes 786440 | tf_op jit(solution)/shard_map/ppermute | solution.py:183
  59.0 13.1 %collective-permute-start.6 = (bf16[1024,128]{1,0:T(8,128)(2,1)S(1)}, bf16[1024,128]{1,0:T(8,128)(2,1)S(1)}, u32[]{:S(2)}, u32[]{:S(2)}) collective-permute-start(bf16[1024,128]{1,0:T(8,128)(2,1)S(1)} %copy-done.14), channel_id=1, source_target_pairs={{0,8},{8,0},{16,24},{24,16},{32,40},{40,32},{48,56},{56,48},{64,72... | collective-permute-start | bytes 786440 | tf_op jit(solution)/shard_map/ppermute | solution.py:46
  59.5 13.1 %collective-permute-start.23 = (bf16[256,512]{1,0:T(8,128)(2,1)S(1)}, bf16[256,512]{1,0:T(8,128)(2,1)S(1)}, u32[]{:S(2)}, u32[]{:S(2)}) collective-permute-start(bf16[256,512]{1,0:T(8,128)(2,1)S(1)} %collective-permute-done.21.u1), channel_id=1, source_target_pairs={{0,1},{1,2},{2,3},{3,4},{4,5},{5,6},{6,7},{7,0},{8,9},{9,10},{10,1... | collective-permute-start | bytes 786440 | tf_op jit(solution)/shard_map/ppermute | solution.py:206
  70.7 10.4 %collective-permute-start.17 = (bf16[1024,128]{1,0:T(8,128)(2,1)S(1)}, bf16[1024,128]{1,0:T(8,128)(2,1)S(1)}, u32[]{:S(2)}, u32[]{:S(2)}) collective-permute-start(bf16[1024,128]{1,0:T(8,128)(2,1)S(1)} %collective-permute-done.13), channel_id=1, source_target_pairs={{0,8},{8,0},{16,24},{24,16},{32,40},{40,32},{48,56},{56,48},{64,72... | collective-permute-start | bytes 786440 | tf_op jit(solution)/shard_map/ppermute | solution.py:46
  71.9 12.1 %collective-permute-start.18 = (bf16[1024,128]{1,0:T(8,128)(2,1)S(1)}, bf16[1024,128]{1,0:T(8,128)(2,1)S(1)}, u32[]{:S(2)}, u32[]{:S(2)}) collective-permute-start(bf16[1024,128]{1,0:T(8,128)(2,1)S(1)} %collective-permute-done.14), channel_id=1, source_target_pairs={{0,8},{8,0},{16,24},{24,16},{32,40},{40,32},{48,56},{56,48},{64,72... | collective-permute-start | bytes 786440 | tf_op jit(solution)/shard_map/ppermute | solution.py:46
  72.1 15.4 %collective-permute-start.19 = (bf16[1024,128]{1,0:T(8,128)(2,1)S(1)}, bf16[1024,128]{1,0:T(8,128)(2,1)S(1)}, u32[]{:S(2)}, u32[]{:S(2)}) collective-permute-start(bf16[1024,128]{1,0:T(8,128)(2,1)S(1)} %collective-permute-done.15), channel_id=1, source_target_pairs={{0,8},{8,0},{16,24},{24,16},{32,40},{40,32},{48,56},{56,48},{64,72... | collective-permute-start | bytes 786440 | tf_op jit(solution)/shard_map/ppermute | solution.py:46
  72.7 11.2 %collective-permute-start.25 = (bf16[256,512]{1,0:T(8,128)(2,1)S(1)}, bf16[256,512]{1,0:T(8,128)(2,1)S(1)}, u32[]{:S(2)}, u32[]{:S(2)}) collective-permute-start(bf16[256,512]{1,0:T(8,128)(2,1)S(1)} %collective-permute-done.23.u3), channel_id=1, source_target_pairs={{0,1},{1,2},{2,3},{3,4},{4,5},{5,6},{6,7},{7,0},{8,9},{9,10},{10,1... | collective-permute-start | bytes 786440 | tf_op jit(solution)/shard_map/ppermute | solution.py:206
  81.1 15.3 %collective-permute-start.20 = (bf16[1024,128]{1,0:T(8,128)(2,1)S(1)}, bf16[1024,128]{1,0:T(8,128)(2,1)S(1)}, u32[]{:S(2)}, u32[]{:S(2)}) collective-permute-start(bf16[1024,128]{1,0:T(8,128)(2,1)S(1)} %bitcast.22), channel_id=1, source_target_pairs={{0,8},{8,0},{16,24},{24,16},{32,40},{40,32},{48,56},{56,48},{64,72... | collective-permute-start | bytes 786440 | tf_op jit(solution)/shard_map/ppermute | solution.py:46
  83.9 9.8 %collective-permute-start.7 = (bf16[1024,128]{1,0:T(8,128)(2,1)S(1)}, bf16[1024,128]{1,0:T(8,128)(2,1)S(1)}, u32[]{:S(2)}, u32[]{:S(2)}) collective-permute-start(bf16[1024,128]{1,0:T(8,128)(2,1)S(1)} %collective-permute-done.3), channel_id=1, source_target_pairs={{0,8},{8,0},{16,24},{24,16},{32,40},{40,32},{48,56},{56,48},{64,72... | collective-permute-start | bytes 786440 | tf_op jit(solution)/shard_map/ppermute | solution.py:46
  84.0 8.3 %collective-permute-start.28 = (bf16[128,512]{1,0:T(8,128)(2,1)S(1)}, bf16[128,512]{1,0:T(8,128)(2,1)S(1)}, u32[]{:S(2)}, u32[]{:S(2)}) collective-permute-start(bf16[128,512]{1,0:T(8,128)(2,1)S(1)} %slice.25), channel_id=1, source_target_pairs={{0,7},{1,0},{2,1},{3,2},{4,3},{5,4},{6,5},{7,6},{8,15},{9,8},{10,9... | collective-permute-start | bytes 393224 | tf_op jit(solution)/shard_map/ppermute | solution.py:209
  103.1 38.9 %all-to-all-start = ((bf16[16,256,256]{2,1,0:T(8,128)(2,1)}), bf16[16,256,256]{2,1,0:T(8,128)(2,1)S(1)}, u32[]{:S(2)}, u32[]{:S(2)}) async-start(bf16[16,256,256]{2,1,0:T(8,128)(2,1)} %bitcast.27), calls=%async_computation | async-start | bytes 4194304 | tf_op jit(solution)/shard_map/all_to_all | solution.py:337
  (26 other events, 239.2 us)

commit v2 on v1

v2 whole, which is shorter than its diff:
```python
import math

import jax
import jax.numpy as jnp
from jax import lax
from jax.experimental import pallas as pl
from jax.experimental.pallas import tpu as pltpu
from jax.sharding import PartitionSpec as P

HD = 128
GROUP = 4
SIDE = 4
CHIPS = SIDE * SIDE
HEADS = 8
BLOCKS = 64
MINE = BLOCKS // 2
STACK = GROUP * HD
FACTOR = 1.0 / math.sqrt(HD)
LOG2E = math.log2(math.e)

NT = (((1,), (1,)), ((), ()))
TN = (((0,), (0,)), ((), ()))
NN = (((1,), (0,)), ((), ()))

SWAP = [(i, i ^ 1) for i in range(2 * CHIPS)]
SAME_CORE = [[2 * c + k for c in range(CHIPS)] for k in range(2)]


def chip_shift(dx, dy):
    pairs = []
    for x in range(SIDE):
        for y in range(SIDE):
            target = ((x + dx) % SIDE) * SIDE + (y + dy) % SIDE
            for core in range(2):
                pairs.append(((x * SIDE + y) * 2 + core, target * 2 + core))
    return pairs


def head_shift(by):
    return [(i, (i + by) % HEADS) for i in range(HEADS)]


def swapped(value):
    return lax.ppermute(value, "seq", SWAP)


def vmem():
    return pl.BlockSpec(memory_space=pltpu.VMEM)


def smem():
    return pl.BlockSpec(memory_space=pltpu.SMEM)


def project_first(_bound, own, forth_1, back_1, forth_2, back_2, weight, total_ref, later_ref, held, sems):
    me = lax.axis_index("head")
    depth = held.shape[2]
    offsets = (0, -1, 1, -2, 2, -3, 3, 4)

    def fetch(n):
        source = lax.rem(me + offsets[n] + HEADS, HEADS)
        columns = pl.ds(pl.multiple_of(source * depth, depth), depth)
        target = held.at[n] if n < 5 else later_ref.at[n - 5]
        return pltpu.make_async_copy(weight.at[:, columns], target, sems.at[n])

    for n in range(8):
        fetch(n).start()
    total = jnp.zeros(total_ref.shape, jnp.float32)
    for n, rows in enumerate((own, forth_1, back_1, forth_2, back_2)):
        fetch(n).wait()
        total += lax.dot_general(rows[...], held[n], NT, preferred_element_type=jnp.float32)
    total_ref[...] = total
    for n in range(5, 8):
        fetch(n).wait()


def project_last(total_ref, forth_3, back_3, top, bottom, weight, attention_ref, grad_ref, delta_ref):
    for slot, far in ((0, top), (1, bottom)):
        rows = slice(slot * HD, (slot + 1) * HD)
        total = total_ref[rows, :]
        for n, part in enumerate((forth_3[rows, :], back_3[rows, :], far[...])):
            total += lax.dot_general(part, weight[n], NT, preferred_element_type=jnp.float32)
        grad = total.astype(jnp.bfloat16)
        products = grad.astype(jnp.float32) * attention_ref[rows, :].astype(jnp.float32)
        for g in range(GROUP):
            columns = slice(g * HD, (g + 1) * HD)
            grad_ref[slot * STACK + g * HD : slot * STACK + (g + 1) * HD, :] = grad[:, columns]
            delta_ref[slot, :, columns] = jnp.sum(
                jnp.transpose(products[:, columns]), axis=0, keepdims=True
            )


def plan(lengths, owners, position, slot, bound, place, target, before):
    me = lax.axis_index("seq")
    core = me & 1
    my_x, my_y = me >> 3, (me >> 1) & 3

    def invert(i, carry):
        target[owners[i]] = i
        return carry

    lax.fori_loop(0, BLOCKS, invert, 0, unroll=8)

    def visit(t, n):
        row = jnp.where(t < MINE, 2 * t, 2 * (BLOCKS - 1 - t) + 1)
        goal = target[row]
        mine = ((goal >> 1) & 1) == core
        before[t] = n
        position[n] = t
        slot[n] = (goal >> 2) * 2 + (goal & 1)
        far = jnp.where(((row >> 1) & 1) == core, 0, MINE)
        back_x = (my_x - (row >> 4) + SIDE) & 3
        back_y = (my_y - ((row >> 2) & 3) + SIDE) & 3
        place[far + back_x * 8 + back_y * 2 + (row & 1)] = jnp.where(mine, n, MINE)
        return n + mine.astype(jnp.int32)

    before[BLOCKS] = lax.fori_loop(0, BLOCKS, visit, jnp.int32(0), unroll=8)
    position[MINE] = 4 * BLOCKS
    for q, top in enumerate((me, BLOCKS - 1 - me, me ^ 1, BLOCKS - 1 - (me ^ 1))):
        end = start = jnp.int32(0)
        for d in range(lengths.shape[0]):
            end = end + lengths[d]
            start = jnp.where(end <= top * HD, end, start)
        bound[2 * q] = before[start >> 7]
        bound[2 * q + 1] = before[top + 1]


def tip(forth, back, top, bottom):
    top[...] = forth[:HD, :]
    bottom[...] = back[HD:, :]


def join(*refs):
    rows = refs[0].shape[0]
    for n in range(SIDE):
        refs[-1][n * rows : (n + 1) * rows, :] = refs[n][...]


def halve(forth, back, *refs):
    rows = refs[-1].shape[0]
    refs[-2][...] = forth[:rows, :]
    refs[-1][...] = back[rows:, :]


def sort_keys(place, *refs):
    pieces, (sorted_keys, sorted_values) = refs[:-2], refs[-2:]
    firsts = [side + first for side in (0, MINE) for first in (0, 8, 24, 16, 20)]
    goals = [place[n] for n in range(BLOCKS)]
    for first, piece in zip(firsts, pieces):
        for n in range(piece.shape[0] // HD):
            goal = pl.ds(pl.multiple_of(goals[first + n] * HD, HD), HD)
            rows = slice(n * HD, (n + 1) * HD)
            sorted_keys[goal, :] = piece[rows, :HD]
            sorted_values[goal, :] = piece[rows, HD:]
    for out in (sorted_keys, sorted_values):
        out[MINE * HD :, :] = jnp.zeros((HD, HD), jnp.bfloat16)


def attend(
    lengths,
    position_ref,
    slot_ref,
    bound_ref,
    keys_ref,
    values_ref,
    q_own,
    q_sib,
    do_own,
    do_sib,
    norm_own,
    norm_sib,
    delta_own,
    delta_sib,
    parts_ref,
    dq_own,
    dq_sib,
    dk_ref,
    dv_ref,
    dqt_ref,
    q_ref,
    do_ref,
):
    me = lax.axis_index("seq")
    dk_ref[...] = jnp.zeros_like(dk_ref)
    dv_ref[...] = jnp.zeros_like(dv_ref)
    upper = lax.broadcasted_iota(jnp.int32, (2 * HD, 1), 0)
    lane = lax.broadcasted_iota(jnp.int32, (1, 2 * STACK), 1)
    for slot in range(2):
        rows = slice(slot * HD, (slot + 1) * HD)
        for side, (queries, grads) in enumerate(((q_own, do_own), (q_sib, do_sib))):
            for g in range(GROUP):
                at = side * STACK + g * HD
                q_ref[at : at + HD, :] = queries[rows, g * HD : (g + 1) * HD]
            do_ref[side * STACK : (side + 1) * STACK, :] = grads[slot * STACK : (slot + 1) * STACK, :]
        norm = LOG2E * jnp.concatenate(
            [norms[g : g + 1, rows] for norms in (norm_own, norm_sib) for g in range(GROUP)], axis=1
        )
        delta = jnp.concatenate([delta_own[slot], delta_sib[slot]], axis=1)
        tops = [other if slot == 0 else BLOCKS - 1 - other for other in (me, me ^ 1)]
        last = jnp.where(lane < STACK, tops[0] * HD, tops[1] * HD) + (lane & (HD - 1))
        end = jnp.int32(0)
        first = jnp.zeros_like(last)
        for d in range(lengths.shape[0]):
            end = end + lengths[d]
            first = jnp.where(end <= last, end, first)
        begin = jnp.minimum(bound_ref[2 * slot], bound_ref[2 * slot + 4])
        stop = jnp.maximum(bound_ref[2 * slot + 1], bound_ref[2 * slot + 5])
        dqt_ref[...] = jnp.zeros_like(dqt_ref)

        def visit(step, carry):
            index = begin + 2 * step
            here = pl.ds(pl.multiple_of(index * HD, HD), 2 * HD)
            keys = keys_ref[here, :]
            queries = q_ref[...]
            grads = do_ref[...]
            low = position_ref[index] * HD
            high = (position_ref[index + 1] - 1) * HD
            place = upper + jnp.where(upper < HD, low, high)
            scores = lax.dot_general(keys, queries, NT, preferred_element_type=jnp.float32)
            prob_grad = lax.dot_general(
                values_ref[here, :], grads, NT, preferred_element_type=jnp.float32
            )
            allowed = (place >= first) & (place <= last)
            weights = jnp.where(allowed, jnp.exp2(scores * (FACTOR * LOG2E) - norm), 0.0)
            score_grad = (weights * (prob_grad - delta)).astype(jnp.bfloat16)
            dv_ref[here, :] += lax.dot_general(
                weights.astype(jnp.bfloat16), grads, NN, preferred_element_type=jnp.float32
            )
            dk_ref[here, :] += lax.dot_general(
                score_grad, queries, NN, preferred_element_type=jnp.float32
            )
            dqt_ref[...] += lax.dot_general(
                keys, score_grad, TN, preferred_element_type=jnp.float32
            )
            return carry

        lax.fori_loop(0, (stop - begin + 1) >> 1, visit, 0)
        for side, out in enumerate((dq_own, dq_sib)):
            for g in range(GROUP):
                at = side * STACK + g * HD
                out[rows, g * HD : (g + 1) * HD] = (
                    jnp.transpose(dqt_ref[:, at : at + HD]) * FACTOR
                )

    def hand_out(n, carry):
        source = pl.ds(pl.multiple_of(n * HD, HD), HD)
        target = pl.ds(pl.multiple_of(slot_ref[n] * HD, HD), HD)
        parts_ref[target, :HD] = (dk_ref[source, :] * FACTOR).astype(jnp.bfloat16)
        parts_ref[target, HD:] = dv_ref[source, :].astype(jnp.bfloat16)
        return carry

    lax.fori_loop(0, MINE, hand_out, 0, unroll=2)


def anywhere():
    return pl.BlockSpec(memory_space=pl.ANY)


def array(shape, dtype):
    return jax.ShapeDtypeStruct(shape, dtype)


def call(body, outs, ins, out_specs, flops, moved, scratch=(), room=16):
    return pl.pallas_call(
        body,
        out_shape=outs,
        in_specs=ins,
        out_specs=out_specs,
        scratch_shapes=scratch,
        compiler_params=pltpu.CompilerParams(vmem_limit_bytes=room << 20),
        cost_estimate=pl.CostEstimate(flops=flops, bytes_accessed=moved, transcendentals=0),
        name=body.__name__,
    )


def per_device(
    query_heads,
    key_heads,
    value_heads,
    attention_out,
    log_norm,
    upstream,
    output_weight,
    document_lengths,
    block_owners,
):
    tokens, width = upstream.shape
    bf16, f32, i32 = jnp.bfloat16, jnp.float32, jnp.int32

    def along(axis, value, by):
        if axis == "z":
            return lax.ppermute(value, "head", head_shift(by))
        return lax.ppermute(value, "seq", chip_shift(by, 0) if axis == "x" else chip_shift(0, by))

    position, slot, bound, place = call(
        plan,
        (array((40,), i32), array((40,), i32), array((8,), i32), array((64,), i32)),
        [smem()] * 2,
        [smem()] * 4,
        0,
        1 << 20,
        [pltpu.SMEM((BLOCKS,), i32), pltpu.SMEM((BLOCKS + 8,), i32)],
    )(document_lengths, block_owners)

    pair = jnp.concatenate([key_heads, value_heads], axis=1)
    near = [pair, *[along("y", pair, by) for by in (1, 3, 2)]]
    forth, back = [upstream], [upstream]
    for _ in range(3):
        forth.append(along("z", forth[-1], 1))
        back.append(along("z", back[-1], -1))
    q_sib, norm_sib = swapped(query_heads), swapped(log_norm)

    bundle_0 = call(
        join,
        array((SIDE * tokens, 2 * HD), bf16),
        [vmem()] * 4 + [smem()],
        vmem(),
        30_000_000_000,
        1 << 20,
    )(near[0], near[1], near[3], near[2], bound)
    bundle_1, bundle_3 = along("x", bundle_0, 1), along("x", bundle_0, -1)

    total, later = call(
        project_first,
        (array((tokens, STACK), f32), array((3, STACK, width), bf16)),
        [smem()] + [vmem()] * 5 + [anywhere()],
        [vmem()] * 2,
        10_000_000_000,
        6 << 20,
        [pltpu.VMEM((5, STACK, width), bf16), pltpu.SemaphoreType.DMA((8,))],
    )(bound, upstream, forth[1], back[1], forth[2], back[2], output_weight)

    half = array((SIDE * tokens // 2, 2 * HD), bf16)
    halves = call(
        halve, (half, half), [vmem()] * 2, [vmem()] * 2, 30_000_000_000, 1 << 20
    )(bundle_1, bundle_3)
    pieces = [bundle_0, bundle_1, bundle_3, along("x", halves[0], 1), along("x", halves[1], -1)]

    quarter = array((tokens // 2, width), bf16)
    tips = call(
        tip, (quarter, quarter), [vmem()] * 2, [vmem()] * 2, 0, 1 << 20
    )(forth[3], back[3])
    top, bottom = along("z", tips[0], 1), along("z", tips[1], -1)
    grads, delta = call(
        project_last,
        (array((2 * STACK, HD), bf16), array((2, 1, STACK), f32)),
        [vmem()] * 7,
        [vmem()] * 2,
        2 * tokens * 3 * width * STACK,
        3 << 20,
    )(total, forth[3], back[3], top, bottom, later, attention_out)

    in_order = array(((MINE + 1) * HD, HD), bf16)
    keys, values = call(
        sort_keys, (in_order, in_order), [smem()] + [vmem()] * 10, [vmem()] * 2, 0, 6 << 20
    )(place, *pieces, *map(swapped, pieces))

    parts, dq_own, dq_sib = call(
        attend,
        (array((MINE * HD, 2 * HD), bf16), array((tokens, STACK), f32), array((tokens, STACK), f32)),
        [smem()] * 4 + [vmem()] * 10,
        [vmem()] * 3,
        35 * 10 * GROUP * HD**3,
        8 << 20,
        [
            pltpu.VMEM(((MINE + 1) * HD, HD), f32),
            pltpu.VMEM(((MINE + 1) * HD, HD), f32),
            pltpu.VMEM((HD, 2 * STACK), f32),
            pltpu.VMEM((2 * STACK, HD), bf16),
            pltpu.VMEM((2 * STACK, HD), bf16),
        ],
        28,
    )(
        document_lengths, position, slot, bound, keys, values, query_heads, q_sib,
        grads, swapped(grads), log_norm, norm_sib, delta, swapped(delta),
    )
    query_grad = (dq_own + swapped(dq_sib)).astype(bf16)
    received = lax.all_to_all(
        parts.reshape(CHIPS, 2 * HD, 2 * HD), "seq", 0, 0, tiled=True,
        axis_index_groups=SAME_CORE,
    )
    finished = jnp.sum(received.astype(f32), axis=0).astype(bf16)
    return (query_grad, finished[:, :HD], finished[:, HD:])


def solution(mesh):
    placed = (
        P("seq", "head"),
        P("seq", "head"),
        P("seq", "head"),
        P("seq", "head"),
        P("head", "seq"),
        P("seq", "head"),
        P("head", None),
        P(),
        P(),
    )
    return jax.shard_map(
        per_device,
        mesh=mesh,
        in_specs=placed,
        out_specs=(P("seq", "head"), P("seq", "head"), P("seq", "head")),
        check_vma=False,
    )
```

time: 142 us -> 95.5 us (0.67)
  local copies, waits for them, and re-layouts: 23.4 us -> 3.71 us
  starting transfers between devices: 58.6 us -> 43.9 us
  waiting for transfers between devices: 43.8 us -> 31 us
  Pallas kernels: 11.7 us -> 15.2 us
  other arithmetic: 4.44 us -> 1.07 us
    ppermute x20 -> x15, waiting for transfers between devices: 17.6 us -> 1.98 us  [the longest x8 1.96 us: along(): return lax.ppermute(value, 'head', head_shift(by))]
    unnamed x50 -> x17, local copies, waits for them, and re-layouts: 13.1 us -> 2.19 us
    ppermute x13 -> x10, starting transfers between devices: 17.3 us -> 11.1 us  [swapped(): return lax.ppermute(value, 'seq', SWAP)]
    all_to_all x1, starting transfers between devices: 11.9 us -> 7.37 us  [per_device(): lax.all_to_all(parts.reshape(CHIPS, 2 * HD, 2 * HD), 'seq', 0, 0, tiled=T...]
    dynamic_slice x1 -> x0, local copies, waits for them, and re-layouts: 4.01 us -> none  [weight_of(): return lax.dynamic_slice_in_dim(output_weight, source * width, width, 1)]
    ppermute x20 -> x15, starting transfers between devices: 29.4 us -> 25.4 us  [the longest x8 14.8 us: along(): return lax.ppermute(value, 'head', head_shift(by))]
    pallas_call x4 -> x8, Pallas kernels: 11.7 us -> 15.2 us  [the longest x1 7.48 us: per_device(): call(attend, (array((MINE * HD, 2 * HD), bf16), array((tokens, STACK), f3...]
    reshape x3 -> x0, local copies, waits for them, and re-layouts: 2.8 us -> none  [the longest x2 2.72 us: per_device(): query_heads.reshape(2, HD, GROUP, HD).transpose(0, 2, 1, 3)]
  transfers between devices with their start and end apart: 34 -> 26, of which waited for: 5 -> 5; matrix products, arithmetic and copies ran while one was open for 18% -> 3% of each run, Pallas kernels for 4% -> 8%
where the time goes in v2:
time: 95.5 us; the launch traced here: 95.7 us
  starting transfers between devices  43.9 us (46%)
  waiting for transfers between devices  31 us (32%)
  Pallas kernels  15.2 us (16%)
  local copies, waits for them, and re-layouts  3.71 us (4%)
  other arithmetic  1.07 us (1%)
    all_to_all x1, waiting for transfers between devices, per_device(): lax.all_to_all(parts.reshape(CHIPS, 2 * HD, 2 * HD), 'seq', 0, 0, tiled=T...  26.7 us
    ppermute x8, starting transfers between devices, along(): return lax.ppermute(value, 'head', head_shift(by))  14.8 us
    ppermute x10, starting transfers between devices, swapped(): return lax.ppermute(value, 'seq', SWAP)  11.1 us
    ppermute x7, starting transfers between devices, along(): lax.ppermute(value, 'seq', chip_shift(by, 0) if axis == 'x' else chip_shi...  10.6 us
    pallas_call x1, Pallas kernels, per_device(): call(attend, (array((MINE * HD, 2 * HD), bf16), array((tokens, STACK), f3...  7.48 us
    all_to_all x1, starting transfers between devices, per_device(): lax.all_to_all(parts.reshape(CHIPS, 2 * HD, 2 * HD), 'seq', 0, 0, tiled=T...  7.37 us
    pallas_call x1, Pallas kernels, per_device(): call(project_first, (array((tokens, STACK), f32), array((3, STACK, width)...  2.42 us
    ppermute x10, waiting for transfers between devices, swapped(): return lax.ppermute(value, 'seq', SWAP)  2.3 us
  transfers between devices with their start and end apart: 26, of which 5 were waited for; matrix products, arithmetic and copies ran while one was open for 3% of the time, Pallas kernels for 8%

profile of v2, /device:TPU:1, one launch (start us, length us, event | category | flops | bytes accessed | tf_op | source)
XLA Modules:
  0.0 95.7 jit_solution(17704549716081258866)
XLA Ops:
  0.6 2.5 %collective-permute-start.13 = (bf16[256,512]{1,0:T(8,128)(2,1)}, bf16[256,512]{1,0:T(8,128)(2,1)S(1)}, u32[]{:S(2)}, u32[]{:S(2)}) collective-permute-start(bf16[256,512]{1,0:T(8,128)(2,1)} %own.1), channel_id=1, source_target_pairs={{0,1},{1,2},{2,3},{3,4},{4,5},{5,6},{6,7},{7,0},{8,9},{9,10},{10,1... | collective-permute-start | bytes 786440 | tf_op jit(solution)/shard_map/ppermute | solution.py:292
  3.2 4.0 %collective-permute-start.14 = (bf16[256,512]{1,0:T(8,128)(2,1)}, bf16[256,512]{1,0:T(8,128)(2,1)S(1)}, u32[]{:S(2)}, u32[]{:S(2)}) collective-permute-start(bf16[256,512]{1,0:T(8,128)(2,1)} %own.1), channel_id=1, source_target_pairs={{0,7},{1,0},{2,1},{3,2},{4,3},{5,4},{6,5},{7,6},{8,15},{9,8},{10,9... | collective-permute-start | bytes 786440 | tf_op jit(solution)/shard_map/ppermute | solution.py:292
  8.9 1.4 %collective-permute-start = (bf16[256,256]{1,0:T(8,128)(2,1)S(1)}, bf16[256,256]{1,0:T(8,128)(2,1)S(1)}, u32[]{:S(2)}, u32[]{:S(2)}) collective-permute-start(bf16[256,256]{1,0:T(8,128)(2,1)S(1)} %constant_dynamic-update-slice_fusion.refs_0_), channel_id=1, source_target_pairs={{0,16},{8,24},{16,32},{24,40},{32,48},{40,56},{48,0},{56,8},{64,80... | collective-permute-start | bytes 393224 | tf_op jit(solution)/shard_map/ppermute | solution.py:293
  10.3 2.6 %collective-permute-start.1 = (bf16[256,256]{1,0:T(8,128)(2,1)S(1)}, bf16[256,256]{1,0:T(8,128)(2,1)S(1)}, u32[]{:S(2)}, u32[]{:S(2)}) collective-permute-start(bf16[256,256]{1,0:T(8,128)(2,1)S(1)} %constant_dynamic-update-slice_fusion.refs_0_), channel_id=1, source_target_pairs={{0,32},{8,40},{16,48},{24,56},{32,0},{40,8},{48,16},{56,24},{64,96... | collective-permute-start | bytes 393224 | tf_op jit(solution)/shard_map/ppermute | solution.py:293
  12.9 1.1 %collective-permute-start.2 = (bf16[256,256]{1,0:T(8,128)(2,1)S(1)}, bf16[256,256]{1,0:T(8,128)(2,1)S(1)}, u32[]{:S(2)}, u32[]{:S(2)}) collective-permute-start(bf16[256,256]{1,0:T(8,128)(2,1)S(1)} %constant_dynamic-update-slice_fusion.refs_0_), channel_id=1, source_target_pairs={{0,48},{8,56},{16,0},{24,8},{32,16},{40,24},{48,32},{56,40},{64,11... | collective-permute-start | bytes 393224 | tf_op jit(solution)/shard_map/ppermute | solution.py:293
  15.3 2.1 %plan.1 = (s32[40]{0:T(128)S(1)}, s32[40]{0:T(128)S(1)}, s32[8]{0:T(128)S(1)}, s32[64]{0:T(128)S(1)}) custom-call(s32[8]{0:T(128)S(1)} %copy-done.6, s32[64]{0:T(128)S(1)} %copy-done.5), custom_call_target="tpu_custom_call" | custom-call | bytes 1048576 | tf_op jit(solution)/shard_map/plan/pallas_call | solution.py:295
  17.6 2.7 %collective-permute-start.16 = (bf16[256,512]{1,0:T(8,128)(2,1)S(1)}, bf16[256,512]{1,0:T(8,128)(2,1)S(1)}, u32[]{:S(2)}, u32[]{:S(2)}) collective-permute-start(bf16[256,512]{1,0:T(8,128)(2,1)S(1)} %collective-permute-done.14.back_1), channel_id=1, source_target_pairs={{0,7},{1,0},{2,1},{3,2},{4,3},{5,4},{6,5},{7,6},{8,15},{9,8},{10,9... | collective-permute-start | bytes 786440 | tf_op jit(solution)/shard_map/ppermute | solution.py:292
  20.8 1.3 %collective-permute-start.3 = (bf16[1024,256]{1,0:T(8,128)(2,1)S(1)}, bf16[1024,256]{1,0:T(8,128)(2,1)S(1)}, u32[]{:S(2)}, u32[]{:S(2)}) collective-permute-start(bf16[1024,256]{1,0:T(8,128)(2,1)S(1)} %join.1.refs_0_), channel_id=1, source_target_pairs={{0,64},{8,72},{16,80},{24,88},{32,96},{40,104},{48,112},{56,120},{... | collective-permute-start | bytes 1572872 | tf_op jit(solution)/shard_map/ppermute | solution.py:293
  22.1 1.5 %collective-permute-start.4 = (bf16[1024,256]{1,0:T(8,128)(2,1)S(1)}, bf16[1024,256]{1,0:T(8,128)(2,1)S(1)}, u32[]{:S(2)}, u32[]{:S(2)}) collective-permute-start(bf16[1024,256]{1,0:T(8,128)(2,1)S(1)} %join.1.refs_0_), channel_id=1, source_target_pairs={{0,192},{8,200},{16,208},{24,216},{32,224},{40,232},{48,240},{56,2... | collective-permute-start | bytes 1572872 | tf_op jit(solution)/shard_map/ppermute | solution.py:293
  23.6 1.2 %collective-permute-done.15.forth_2 = bf16[256,512]{1,0:T(8,128)(2,1)S(1)} collective-permute-done((bf16[256,512]{1,0:T(8,128)(2,1)S(1)}, bf16[256,512]{1,0:T(8,128)(2,1)S(1)}, u32[]{:S(2)}, u32[]{:S(2)}) %collective-permute-start.15) | collective-permute-done | bytes 262176 | tf_op jit(solution)/shard_map/ppermute | solution.py:292
  24.8 2.7 %collective-permute-start.18 = (bf16[256,512]{1,0:T(8,128)(2,1)S(1)}, bf16[256,512]{1,0:T(8,128)(2,1)S(1)}, u32[]{:S(2)}, u32[]{:S(2)}) collective-permute-start(bf16[256,512]{1,0:T(8,128)(2,1)S(1)} %collective-permute-done.16.back_2), channel_id=1, source_target_pairs={{0,7},{1,0},{2,1},{3,2},{4,3},{5,4},{6,5},{7,6},{8,15},{9,8},{10,9... | collective-permute-start | bytes 786440 | tf_op jit(solution)/shard_map/ppermute | solution.py:292
  27.4 3.3 %collective-permute-start.7 = (bf16[1024,256]{1,0:T(8,128)(2,1)S(1)}, bf16[1024,256]{1,0:T(8,128)(2,1)S(1)}, u32[]{:S(2)}, u32[]{:S(2)}) collective-permute-start(bf16[1024,256]{1,0:T(8,128)(2,1)S(1)} %join.1.refs_0_), channel_id=1, source_target_pairs={{0,8},{8,0},{16,24},{24,16},{32,40},{40,32},{48,56},{56,48},{64,72... | collective-permute-start | bytes 1572872 | tf_op jit(solution)/shard_map/ppermute | solution.py:44
  31.6 2.8 %collective-permute-start.20 = (bf16[128,512]{1,0:T(8,128)(2,1)S(1)}, bf16[128,512]{1,0:T(8,128)(2,1)S(1)}, u32[]{:S(2)}, u32[]{:S(2)}) collective-permute-start(bf16[128,512]{1,0:T(8,128)(2,1)S(1)} %get-tuple-element.30), channel_id=1, source_target_pairs={{0,7},{1,0},{2,1},{3,2},{4,3},{5,4},{6,5},{7,6},{8,15},{9,8},{10,9... | collective-permute-start | bytes 393224 | tf_op jit(solution)/shard_map/ppermute | solution.py:292
  34.4 1.0 %collective-permute-start.5 = (bf16[512,256]{1,0:T(8,128)(2,1)S(1)}, bf16[512,256]{1,0:T(8,128)(2,1)S(1)}, u32[]{:S(2)}, u32[]{:S(2)}) collective-permute-start(bf16[512,256]{1,0:T(8,128)(2,1)S(1)} %get-tuple-element.24), channel_id=1, source_target_pairs={{0,64},{8,72},{16,80},{24,88},{32,96},{40,104},{48,112},{56,120},{... | collective-permute-start | bytes 786440 | tf_op jit(solution)/shard_map/ppermute | solution.py:293
  35.4 1.8 %collective-permute-start.6 = (bf16[512,256]{1,0:T(8,128)(2,1)S(1)}, bf16[512,256]{1,0:T(8,128)(2,1)S(1)}, u32[]{:S(2)}, u32[]{:S(2)}) collective-permute-start(bf16[512,256]{1,0:T(8,128)(2,1)S(1)} %get-tuple-element.25), channel_id=1, source_target_pairs={{0,192},{8,200},{16,208},{24,216},{32,224},{40,232},{48,240},{56,2... | collective-permute-start | bytes 786440 | tf_op jit(solution)/shard_map/ppermute | solution.py:293
  37.2 4.7 %collective-permute-start.8 = (bf16[1024,256]{1,0:T(8,128)(2,1)S(1)}, bf16[1024,256]{1,0:T(8,128)(2,1)S(1)}, u32[]{:S(2)}, u32[]{:S(2)}) collective-permute-start(bf16[1024,256]{1,0:T(8,128)(2,1)S(1)} %collective-permute-done.3.forth.refs_1_), channel_id=1, source_target_pairs={{0,8},{8,0},{16,24},{24,16},{32,40},{40,32},{48,56},{56,48},{64,72... | collective-permute-start | bytes 1572872 | tf_op jit(solution)/shard_map/ppermute | solution.py:44
  42.0 2.4 %project_first.1 = (f32[256,512]{1,0:T(8,128)S(1)}, bf16[3,512,512]{2,1,0:T(8,128)(2,1)S(1)}) custom-call(s32[8]{0:T(128)S(1)} %get-tuple-element.22.refs_4_._bound.bound_ref, bf16[256,512]{1,0:T(8,128)(2,1)S(1)} %copy-done.2, bf16[256,512]{1,0:T(8,128)(2,1)S(1)} %collective-permute-done.13.forth_1, bf16[256,512]{1,0:T(8,128)(2,1)S(1)} %collective-permute-done.14.back_1, ...), custom_call_target="tpu_custom_call" | custom-call | flops 10000000000 | bytes 6291456 | tf_op jit(solution)/shard_map/project_first/pallas_call | solution.py:323
  44.4 1.8 %collective-permute-start.10 = (bf16[512,256]{1,0:T(8,128)(2,1)S(1)}, bf16[512,256]{1,0:T(8,128)(2,1)S(1)}, u32[]{:S(2)}, u32[]{:S(2)}) collective-permute-start(bf16[512,256]{1,0:T(8,128)(2,1)S(1)} %collective-permute-done.5.refs_3_), channel_id=1, source_target_pairs={{0,8},{8,0},{16,24},{24,16},{32,40},{40,32},{48,56},{56,48},{64,72... | collective-permute-start | bytes 786440 | tf_op jit(solution)/shard_map/ppermute | solution.py:44
  46.2 1.2 %project_last.1 = (bf16[1024,128]{1,0:T(8,128)(2,1)S(1)}, f32[2,1,512]{2,1,0:T(1,128)S(1)}) custom-call(f32[256,512]{1,0:T(8,128)S(1)} %get-tuple-element.28.total_ref, bf16[256,512]{1,0:T(8,128)(2,1)S(1)} %collective-permute-done.17.forth.forth_3, bf16[256,512]{1,0:T(8,128)(2,1)S(1)} %collective-permute-done.18.back.back_3, ...), custom_call_target="tpu_custom_call" | custom-call | flops 402653184 | bytes 3145728 | tf_op jit(solution)/shard_map/project_last/pallas_call | solution.py:344
  49.1 1.3 %sort_keys.1 = (bf16[4224,128]{1,0:T(8,128)(2,1)S(1)}, bf16[4224,128]{1,0:T(8,128)(2,1)S(1)}) custom-call(s32[64]{0:T(128)S(1)} %get-tuple-element.23.place, bf16[1024,256]{1,0:T(8,128)(2,1)S(1)} %join.1.refs_0_, bf16[1024,256]{1,0:T(8,128)(2,1)S(1)} %collective-permute-done.3.forth.refs_1_, bf16[1024,256]{1,0:T(8,128)(2,1)S(1)} %collective-permute-done.4.back.refs_2_, ...), custom_call_target="tpu_custom_call" | custom-call | bytes 6291456 | tf_op jit(solution)/shard_map/sort_keys/pallas_call | solution.py:354
  50.4 7.5 %attend.1 = (bf16[4096,256]{1,0:T(8,128)(2,1)}, f32[256,512]{1,0:T(8,128)S(1)}, f32[256,512]{1,0:T(8,128)S(1)}) custom-call(s32[8]{0:T(128)S(1)} %copy-done.7, s32[40]{0:T(128)S(1)} %get-tuple-element.20.position_ref, s32[40]{0:T(128)S(1)} %get-tuple-element.21.slot_ref, s32[8]{0:T(128)S(1)} %get-tuple-element.22.refs_4_._bound.bound_ref, ...), custom_call_target="tpu_custom_call" | custom-call | flops 2936012800 | bytes 8388608 | tf_op jit(solution)/shard_map/attend/pallas_call | solution.py:358
  57.9 7.4 %all-to-all-start = ((bf16[16,256,256]{2,1,0:T(8,128)(2,1)}), bf16[16,256,256]{2,1,0:T(8,128)(2,1)S(1)}, u32[]{:S(2)}, u32[]{:S(2)}) async-start(bf16[16,256,256]{2,1,0:T(8,128)(2,1)} %bitcast), calls=%async_computation | async-start | bytes 4194304 | tf_op jit(solution)/shard_map/all_to_all | solution.py:378
  65.4 1.9 %collective-permute-done.24 = f32[256,512]{1,0:T(8,128)S(1)} collective-permute-done((f32[256,512]{1,0:T(8,128)S(1)}, f32[256,512]{1,0:T(8,128)S(1)}, u32[]{:S(2)}, u32[]{:S(2)}) %collective-permute-start.24) | collective-permute-done | bytes 524320 | tf_op jit(solution)/shard_map/ppermute | solution.py:44
  68.1 26.7 %all-to-all-done = bf16[16,256,256]{2,1,0:T(8,128)(2,1)S(1)} async-done(((bf16[16,256,256]{2,1,0:T(8,128)(2,1)}), bf16[16,256,256]{2,1,0:T(8,128)(2,1)S(1)}, u32[]{:S(2)}, u32[]{:S(2)}) %all-to-all-start) | async-done | bytes 2097184 | tf_op jit(solution)/shard_map/all_to_all | solution.py:378
  (57 shorter events, 8.2 us)
Async XLA Ops:
  0.6 16.8 %collective-permute-start.13 = (bf16[256,512]{1,0:T(8,128)(2,1)}, bf16[256,512]{1,0:T(8,128)(2,1)S(1)}, u32[]{:S(2)}, u32[]{:S(2)}) collective-permute-start(bf16[256,512]{1,0:T(8,128)(2,1)} %own.1), channel_id=1, source_target_pairs={{0,1},{1,2},{2,3},{3,4},{4,5},{5,6},{6,7},{7,0},{8,9},{9,10},{10,1... | collective-permute-start | bytes 786440 | tf_op jit(solution)/shard_map/ppermute | solution.py:292
  3.2 14.4 %collective-permute-start.14 = (bf16[256,512]{1,0:T(8,128)(2,1)}, bf16[256,512]{1,0:T(8,128)(2,1)S(1)}, u32[]{:S(2)}, u32[]{:S(2)}) collective-permute-start(bf16[256,512]{1,0:T(8,128)(2,1)} %own.1), channel_id=1, source_target_pairs={{0,7},{1,0},{2,1},{3,2},{4,3},{5,4},{6,5},{7,6},{8,15},{9,8},{10,9... | collective-permute-start | bytes 786440 | tf_op jit(solution)/shard_map/ppermute | solution.py:292
  8.9 11.3 %collective-permute-start = (bf16[256,256]{1,0:T(8,128)(2,1)S(1)}, bf16[256,256]{1,0:T(8,128)(2,1)S(1)}, u32[]{:S(2)}, u32[]{:S(2)}) collective-permute-start(bf16[256,256]{1,0:T(8,128)(2,1)S(1)} %constant_dynamic-update-slice_fusion.refs_0_), channel_id=1, source_target_pairs={{0,16},{8,24},{16,32},{24,40},{32,48},{40,56},{48,0},{56,8},{64,80... | collective-permute-start | bytes 393224 | tf_op jit(solution)/shard_map/ppermute | solution.py:293
  10.3 9.9 %collective-permute-start.1 = (bf16[256,256]{1,0:T(8,128)(2,1)S(1)}, bf16[256,256]{1,0:T(8,128)(2,1)S(1)}, u32[]{:S(2)}, u32[]{:S(2)}) collective-permute-start(bf16[256,256]{1,0:T(8,128)(2,1)S(1)} %constant_dynamic-update-slice_fusion.refs_0_), channel_id=1, source_target_pairs={{0,32},{8,40},{16,48},{24,56},{32,0},{40,8},{48,16},{56,24},{64,96... | collective-permute-start | bytes 393224 | tf_op jit(solution)/shard_map/ppermute | solution.py:293
  12.9 7.3 %collective-permute-start.2 = (bf16[256,256]{1,0:T(8,128)(2,1)S(1)}, bf16[256,256]{1,0:T(8,128)(2,1)S(1)}, u32[]{:S(2)}, u32[]{:S(2)}) collective-permute-start(bf16[256,256]{1,0:T(8,128)(2,1)S(1)} %constant_dynamic-update-slice_fusion.refs_0_), channel_id=1, source_target_pairs={{0,48},{8,56},{16,0},{24,8},{32,16},{40,24},{48,32},{56,40},{64,11... | collective-permute-start | bytes 393224 | tf_op jit(solution)/shard_map/ppermute | solution.py:293
  17.5 7.3 %collective-permute-start.15 = (bf16[256,512]{1,0:T(8,128)(2,1)S(1)}, bf16[256,512]{1,0:T(8,128)(2,1)S(1)}, u32[]{:S(2)}, u32[]{:S(2)}) collective-permute-start(bf16[256,512]{1,0:T(8,128)(2,1)S(1)} %collective-permute-done.13.forth_1), channel_id=1, source_target_pairs={{0,1},{1,2},{2,3},{3,4},{4,5},{5,6},{6,7},{7,0},{8,9},{9,10},{10,1... | collective-permute-start | bytes 786440 | tf_op jit(solution)/shard_map/ppermute | solution.py:292
  17.6 7.2 %collective-permute-start.16 = (bf16[256,512]{1,0:T(8,128)(2,1)S(1)}, bf16[256,512]{1,0:T(8,128)(2,1)S(1)}, u32[]{:S(2)}, u32[]{:S(2)}) collective-permute-start(bf16[256,512]{1,0:T(8,128)(2,1)S(1)} %collective-permute-done.14.back_1), channel_id=1, source_target_pairs={{0,7},{1,0},{2,1},{3,2},{4,3},{5,4},{6,5},{7,6},{8,15},{9,8},{10,9... | collective-permute-start | bytes 786440 | tf_op jit(solution)/shard_map/ppermute | solution.py:292
  20.8 13.6 %collective-permute-start.3 = (bf16[1024,256]{1,0:T(8,128)(2,1)S(1)}, bf16[1024,256]{1,0:T(8,128)(2,1)S(1)}, u32[]{:S(2)}, u32[]{:S(2)}) collective-permute-start(bf16[1024,256]{1,0:T(8,128)(2,1)S(1)} %join.1.refs_0_), channel_id=1, source_target_pairs={{0,64},{8,72},{16,80},{24,88},{32,96},{40,104},{48,112},{56,120},{... | collective-permute-start | bytes 1572872 | tf_op jit(solution)/shard_map/ppermute | solution.py:293
  22.1 12.3 %collective-permute-start.4 = (bf16[1024,256]{1,0:T(8,128)(2,1)S(1)}, bf16[1024,256]{1,0:T(8,128)(2,1)S(1)}, u32[]{:S(2)}, u32[]{:S(2)}) collective-permute-start(bf16[1024,256]{1,0:T(8,128)(2,1)S(1)} %join.1.refs_0_), channel_id=1, source_target_pairs={{0,192},{8,200},{16,208},{24,216},{32,224},{40,232},{48,240},{56,2... | collective-permute-start | bytes 1572872 | tf_op jit(solution)/shard_map/ppermute | solution.py:293
  24.7 6.7 %collective-permute-start.17 = (bf16[256,512]{1,0:T(8,128)(2,1)S(1)}, bf16[256,512]{1,0:T(8,128)(2,1)S(1)}, u32[]{:S(2)}, u32[]{:S(2)}) collective-permute-start(bf16[256,512]{1,0:T(8,128)(2,1)S(1)} %collective-permute-done.15.forth_2), channel_id=1, source_target_pairs={{0,1},{1,2},{2,3},{3,4},{4,5},{5,6},{6,7},{7,0},{8,9},{9,10},{10,1... | collective-permute-start | bytes 786440 | tf_op jit(solution)/shard_map/ppermute | solution.py:292
  24.8 6.7 %collective-permute-start.18 = (bf16[256,512]{1,0:T(8,128)(2,1)S(1)}, bf16[256,512]{1,0:T(8,128)(2,1)S(1)}, u32[]{:S(2)}, u32[]{:S(2)}) collective-permute-start(bf16[256,512]{1,0:T(8,128)(2,1)S(1)} %collective-permute-done.16.back_2), channel_id=1, source_target_pairs={{0,7},{1,0},{2,1},{3,2},{4,3},{5,4},{6,5},{7,6},{8,15},{9,8},{10,9... | collective-permute-start | bytes 786440 | tf_op jit(solution)/shard_map/ppermute | solution.py:292
  27.4 20.2 %collective-permute-start.7 = (bf16[1024,256]{1,0:T(8,128)(2,1)S(1)}, bf16[1024,256]{1,0:T(8,128)(2,1)S(1)}, u32[]{:S(2)}, u32[]{:S(2)}) collective-permute-start(bf16[1024,256]{1,0:T(8,128)(2,1)S(1)} %join.1.refs_0_), channel_id=1, source_target_pairs={{0,8},{8,0},{16,24},{24,16},{32,40},{40,32},{48,56},{56,48},{64,72... | collective-permute-start | bytes 1572872 | tf_op jit(solution)/shard_map/ppermute | solution.py:44
  31.5 5.7 %collective-permute-start.19 = (bf16[128,512]{1,0:T(8,128)(2,1)S(1)}, bf16[128,512]{1,0:T(8,128)(2,1)S(1)}, u32[]{:S(2)}, u32[]{:S(2)}) collective-permute-start(bf16[128,512]{1,0:T(8,128)(2,1)S(1)} %get-tuple-element.29), channel_id=1, source_target_pairs={{0,1},{1,2},{2,3},{3,4},{4,5},{5,6},{6,7},{7,0},{8,9},{9,10},{10,1... | collective-permute-start | bytes 393224 | tf_op jit(solution)/shard_map/ppermute | solution.py:292
  31.6 10.3 %collective-permute-start.20 = (bf16[128,512]{1,0:T(8,128)(2,1)S(1)}, bf16[128,512]{1,0:T(8,128)(2,1)S(1)}, u32[]{:S(2)}, u32[]{:S(2)}) collective-permute-start(bf16[128,512]{1,0:T(8,128)(2,1)S(1)} %get-tuple-element.30), channel_id=1, source_target_pairs={{0,7},{1,0},{2,1},{3,2},{4,3},{5,4},{6,5},{7,6},{8,15},{9,8},{10,9... | collective-permute-start | bytes 393224 | tf_op jit(solution)/shard_map/ppermute | solution.py:292
  34.4 10.0 %collective-permute-start.5 = (bf16[512,256]{1,0:T(8,128)(2,1)S(1)}, bf16[512,256]{1,0:T(8,128)(2,1)S(1)}, u32[]{:S(2)}, u32[]{:S(2)}) collective-permute-start(bf16[512,256]{1,0:T(8,128)(2,1)S(1)} %get-tuple-element.24), channel_id=1, source_target_pairs={{0,64},{8,72},{16,80},{24,88},{32,96},{40,104},{48,112},{56,120},{... | collective-permute-start | bytes 786440 | tf_op jit(solution)/shard_map/ppermute | solution.py:293
  35.4 12.1 %collective-permute-start.6 = (bf16[512,256]{1,0:T(8,128)(2,1)S(1)}, bf16[512,256]{1,0:T(8,128)(2,1)S(1)}, u32[]{:S(2)}, u32[]{:S(2)}) collective-permute-start(bf16[512,256]{1,0:T(8,128)(2,1)S(1)} %get-tuple-element.25), channel_id=1, source_target_pairs={{0,192},{8,200},{16,208},{24,216},{32,224},{40,232},{48,240},{56,2... | collective-permute-start | bytes 786440 | tf_op jit(solution)/shard_map/ppermute | solution.py:293
  37.2 10.9 %collective-permute-start.8 = (bf16[1024,256]{1,0:T(8,128)(2,1)S(1)}, bf16[1024,256]{1,0:T(8,128)(2,1)S(1)}, u32[]{:S(2)}, u32[]{:S(2)}) collective-permute-start(bf16[1024,256]{1,0:T(8,128)(2,1)S(1)} %collective-permute-done.3.forth.refs_1_), channel_id=1, source_target_pairs={{0,8},{8,0},{16,24},{24,16},{32,40},{40,32},{48,56},{56,48},{64,72... | collective-permute-start | bytes 1572872 | tf_op jit(solution)/shard_map/ppermute | solution.py:44
  41.9 6.3 %collective-permute-start.9 = (bf16[1024,256]{1,0:T(8,128)(2,1)S(1)}, bf16[1024,256]{1,0:T(8,128)(2,1)S(1)}, u32[]{:S(2)}, u32[]{:S(2)}) collective-permute-start(bf16[1024,256]{1,0:T(8,128)(2,1)S(1)} %collective-permute-done.4.back.refs_2_), channel_id=1, source_target_pairs={{0,8},{8,0},{16,24},{24,16},{32,40},{40,32},{48,56},{56,48},{64,72... | collective-permute-start | bytes 1572872 | tf_op jit(solution)/shard_map/ppermute | solution.py:44
  44.4 4.2 %collective-permute-start.10 = (bf16[512,256]{1,0:T(8,128)(2,1)S(1)}, bf16[512,256]{1,0:T(8,128)(2,1)S(1)}, u32[]{:S(2)}, u32[]{:S(2)}) collective-permute-start(bf16[512,256]{1,0:T(8,128)(2,1)S(1)} %collective-permute-done.5.refs_3_), channel_id=1, source_target_pairs={{0,8},{8,0},{16,24},{24,16},{32,40},{40,32},{48,56},{56,48},{64,72... | collective-permute-start | bytes 786440 | tf_op jit(solution)/shard_map/ppermute | solution.py:44
  47.6 2.8 %collective-permute-start.12 = (bf16[256,512]{1,0:T(8,128)(2,1)S(1)}, bf16[256,512]{1,0:T(8,128)(2,1)S(1)}, u32[]{:S(2)}, u32[]{:S(2)}) collective-permute-start(bf16[256,512]{1,0:T(8,128)(2,1)S(1)} %copy-done.3), channel_id=1, source_target_pairs={{0,8},{8,0},{16,24},{24,16},{32,40},{40,32},{48,56},{56,48},{64,72... | collective-permute-start | bytes 786440 | tf_op jit(solution)/shard_map/ppermute | solution.py:44
  48.1 2.3 %collective-permute-start.21 = (bf16[1024,128]{1,0:T(8,128)(2,1)S(1)}, bf16[1024,128]{1,0:T(8,128)(2,1)S(1)}, u32[]{:S(2)}, u32[]{:S(2)}) collective-permute-start(bf16[1024,128]{1,0:T(8,128)(2,1)S(1)} %get-tuple-element.32.do_own), channel_id=1, source_target_pairs={{0,8},{8,0},{16,24},{24,16},{32,40},{40,32},{48,56},{56,48},{64,72... | collective-permute-start | bytes 786440 | tf_op jit(solution)/shard_map/ppermute | solution.py:44
  48.2 2.2 %collective-permute-start.22 = (f32[4,256]{1,0:T(4,128)S(1)}, f32[4,256]{1,0:T(4,128)S(1)}, u32[]{:S(2)}, u32[]{:S(2)}) collective-permute-start(f32[4,256]{1,0:T(4,128)S(1)} %copy-done.4), channel_id=1, source_target_pairs={{0,8},{8,0},{16,24},{24,16},{32,40},{40,32},{48,56},{56,48},{64,72... | collective-permute-start | bytes 12296 | tf_op jit(solution)/shard_map/ppermute | solution.py:44
  57.9 36.9 %all-to-all-start = ((bf16[16,256,256]{2,1,0:T(8,128)(2,1)}), bf16[16,256,256]{2,1,0:T(8,128)(2,1)S(1)}, u32[]{:S(2)}, u32[]{:S(2)}) async-start(bf16[16,256,256]{2,1,0:T(8,128)(2,1)} %bitcast), calls=%async_computation | async-start | bytes 4194304 | tf_op jit(solution)/shard_map/all_to_all | solution.py:378
  65.3 2.0 %collective-permute-start.24 = (f32[256,512]{1,0:T(8,128)S(1)}, f32[256,512]{1,0:T(8,128)S(1)}, u32[]{:S(2)}, u32[]{:S(2)}) collective-permute-start(f32[256,512]{1,0:T(8,128)S(1)} %get-tuple-element.35), channel_id=1, source_target_pairs={{0,8},{8,0},{16,24},{24,16},{32,40},{40,32},{48,56},{56,48},{64,72... | collective-permute-start | bytes 1572872 | tf_op jit(solution)/shard_map/ppermute | solution.py:44
  (10 other events, 44.6 us)
